TPU v7x, 512 devices: a whole 4x8x8 slice. The times are simulated.
512 devices in a mesh: cand: 16 (over x, z_lo), prompt: 4 (over z_hi, core), tensor: 8 (over y).
Axes of the slice: x: 4, y: 8, z: 8 (z_hi: 2, z_lo: 4; z = z_hi * 4 + z_lo), core: 2. Of those that a mesh axis runs over, the one named last changes fastest.
Arguments:
- owner_index: int32 [4], P('prompt'), may hold values from 0 to 15
- suffix_lengths: int32 [4, 16], P('prompt', 'cand'), may hold values from 64 to 256, as said below
- queries: bfloat16 [4, 4096, 8192], P('prompt', 'cand', 'tensor'), may hold values from -15 to 15
- suffix_kv: bfloat16 [2, 4, 4096, 1024], P(None, 'prompt', 'cand', 'tensor'), may hold values from -6 to 6
- prompt_cache: bfloat16 [2, 4, 16, 4096, 1024], P(None, 'prompt', 'cand', None, 'tensor'), may hold values from -6 to 6
- out_weight: bfloat16 [8192, 4096], P('tensor', 'prompt'), may hold values from -0.09375 to 0.09375
Outputs:
- projected: bfloat16 [4, 4096, 4096], P(None, 'cand', ('prompt', 'tensor'))
Inputs may be any that keep to these rules, and one draw needn't show every extreme that they name: `suffix_lengths`: the first candidate of every prompt has all 256 suffix tokens live.
All inputs are finite; a program needn't handle non-finite values.
Results may differ from a plain program's by a relative error of at most 0.0057.
Values may be sent and summed in bfloat16 or wider, within the bound.
No kernel may reach another device: no remote copies, remote signals or barrier semaphores. Data moves between devices by JAX's collectives and lax.ppermute only.
A program may use at most 64 MiB of HBM per device.

v0:
```python
import math

import jax
import jax.numpy as jnp
from jax import lax
from jax.sharding import PartitionSpec as P

HD = 128
SUF = 256


def spread(value, axis, source):
    kept = jnp.where(lax.axis_index(axis) == source, value, 0).astype(value.dtype)
    return lax.psum(kept, axis)


def attend_blocks(query_rows, key_rows, value_rows, length):
    row_count = query_rows.shape[0]
    key_count = key_rows.shape[0]
    kv_count = key_rows.shape[1] // HD
    group_size = query_rows.shape[1] // (kv_count * HD)
    head_step = math.gcd(group_size, max(1, 512 // row_count))
    score_scale = 1.0 / math.sqrt(HD)
    position = jnp.arange(head_step * row_count, dtype=jnp.int32) % row_count
    column = jnp.arange(key_count, dtype=jnp.int32) - (key_count - row_count)
    allowed = (column[None, :] < 0) | (column[None, :] <= position[:, None]) & (
        column[None, :] < length
    )
    query_heads = query_rows
    query_heads = query_heads.reshape(row_count, group_size, HD).transpose(1, 0, 2)
    query_heads = query_heads.reshape(group_size // head_step, head_step * row_count, HD)

    def head_block(query_block):
        scores = (
            jnp.einsum("qd,kd->qk", query_block, key_rows, preferred_element_type=jnp.float32)
            * score_scale
        )
        scores = jnp.where(allowed, scores, -1e30)
        row_max = jnp.max(scores, axis=-1, keepdims=True)
        exponent = jnp.exp(scores - row_max)
        weights = (exponent / jnp.sum(exponent, axis=-1, keepdims=True)).astype(jnp.bfloat16)
        return jnp.dot(weights, value_rows, preferred_element_type=jnp.float32).astype(jnp.bfloat16)

    finished = lax.map(head_block, query_heads)
    finished = finished.reshape(group_size, row_count, HD).transpose(1, 0, 2)
    pieces = finished.reshape(row_count, group_size * HD)
    return pieces


def body(owner_index, suffix_lengths, queries, suffix_kv, prompt_cache, out_weight):
    prompt_slot = spread(prompt_cache[:, 0, 0], "cand", owner_index[0])
    query_rows = queries[0, 0:SUF]
    suffix_part = suffix_kv[:, 0, 0:SUF]
    key_rows = jnp.concatenate([prompt_slot[0], suffix_part[0]], axis=0)
    value_rows = jnp.concatenate([prompt_slot[1], suffix_part[1]], axis=0)
    outputs = attend_blocks(query_rows, key_rows, value_rows, suffix_lengths[0, 0])
    row_count = outputs.shape[0]
    prompt_count = lax.axis_size("prompt")
    tensor_count = lax.axis_size("tensor")
    partial_value = jnp.dot(
        outputs,
        lax.all_gather(out_weight, "prompt", axis=1, tiled=True),
        preferred_element_type=jnp.float32,
    )
    col_count = partial_value.shape[1] // (prompt_count * tensor_count)
    partial_value = partial_value.reshape(row_count, prompt_count, tensor_count, col_count)
    summed = lax.psum_scatter(partial_value, "tensor", scatter_dimension=2, tiled=True).astype(
        jnp.bfloat16
    )
    exchanged = lax.all_to_all(
        summed.reshape(1, row_count, prompt_count, col_count),
        "prompt",
        split_axis=2,
        concat_axis=0,
        tiled=True,
    )
    return exchanged.reshape(prompt_count, row_count, col_count)


def solution(mesh):
    in_specs = (
        P("prompt"),
        P("prompt", "cand"),
        P("prompt", "cand", "tensor"),
        P(None, "prompt", "cand", "tensor"),
        P(None, "prompt", "cand", None, "tensor"),
        P("tensor", "prompt"),
    )
    out_specs = P(None, "cand", ("prompt", "tensor"))
    return jax.shard_map(body, mesh=mesh, in_specs=in_specs, out_specs=out_specs, check_vma=False)
```

profile of v0, /device:TPU:1, one launch (start us, length us, event | category | flops | bytes accessed | tf_op | source)
XLA Modules:
  0.0 444.1 jit_solution(8244662639623760772)
XLA Ops:
  8.0 3.0 fusion.10
  11.1 0.0 all-reduce.4.cloned.1.call-update
  11.1 0.0 all-gather.2.cloned.1.call-start
  11.1 0.5 all-gather.2.cloned.1.call-update
  12.3 0.1 copy.19
  12.4 0.1 copy.11
  12.5 1.3 dynamic-slice
  13.9 263.5 %all-reduce.4.cloned.1.call-done = bf16[2,4096,128]{2,1,0:T(8,128)(2,1)} async-done(((bf16[2,4096,128]{2,1,0:T(8,128)(2,1)}), bf16[2,4096,128]{2,1,0:T(8,128)(2,1)}) %all-reduce.4.cloned.1.call-update) | async-done | bytes 2097168 | tf_op jit(solution)/shard_map/psum | solution.py:14
  277.4 1.7 slice_bitcast_fusion
  279.1 0.1 pad_maximum_fusion
  279.2 26.0 %while.11 = (s32[]{:T(128)}, bf16[4,512,128]{2,1,0:T(8,128)(2,1)S(1)}, bf16[4,512,128]{2,1,0:T(8,128)(2,1)S(1)}, bf16[4352,128]{1,0:T(8,128)(2,1)S(1)}, bf16[435...) while((s32[]{:T(128)}, ...), condition=%wide.region_4.5_spmd.clone, body=%wide.region_1.4_spmd.clone.sunk | while | flops 1165425664 | bytes 29272172 | solution.py:44
  279.3 2.8 fusion.30
  282.0 1.4 fusion.31
  283.4 2.4 fusion.32
  285.7 2.8 fusion.30
  288.5 1.4 fusion.31
  289.9 2.4 fusion.32
  292.2 2.8 fusion.30
  295.0 1.4 fusion.31
  296.4 2.4 fusion.32
  298.7 2.8 fusion.30
  301.5 1.4 fusion.31
  302.8 2.4 fusion.32
  305.2 0.3 copy.13
  305.6 0.2 reshape.53
  305.8 0.0 all-gather.2.cloned.1.call-done
  305.8 12.0 %copy.14 = bf16[4096,1024]{1,0:T(8,128)(2,1)} copy(bf16[4096,1024]{0,1:T(8,128)(2,1)} %bitcast.70) | data formatting | bytes 16777216 | tf_op jit(solution)/shard_map/dot_general | solution.py:60
  317.8 10.5 %fusion.11 = f32[256,4,8,128]{3,0,2,1:T(8,128)} fusion(bf16[4,8,128,1024]{3,2,1,0:T(8,128)(2,1)} %bitcast.71, bf16[256,1024,1,1]{1,0,2,3:T(8,128)(2,1)S(1)} %reshape.53), kind=kOutput, calls=%fused_computation.19 | convolution fusion | flops 2147483648 | bytes 13107200 | tf_op jit(solution)/shard_map/dot_general | solution.py:60
  328.3 78.4 %all-reduce.5 = bf16[256,4,8,128]{3,0,2,1:T(8,128)(2,1)S(1)} all-reduce(f32[256,4,8,128]{3,0,2,1:T(8,128)} %fusion.11), channel_id=2, replica_groups=mesh['cand'=16,'prompt'=4,'tensor'=8] {'tensor'}, use_global_device_ids=true, to_apply=%region_5.6.clone | all-reduce | flops 1048576 | bytes 6291456
  406.6 0.7 fusion.13
  407.3 28.7 %all_to_all.15 = bf16[1,256,4,128]{3,1,0,2:T(8,128)(2,1)S(1)} all-to-all(bf16[1,256,4,128]{3,1,0,2:T(8,128)(2,1)S(1)} %fusion.13), channel_id=1, replica_groups=mesh['cand'=16,'prompt'=4,'tensor'=8] {'prompt'}, dimensions={2} | all-to-all | bytes 524288 | tf_op jit(solution)/shard_map/all_to_all | solution.py:70
  436.0 0.7 copy.35
  (10 shorter events, 0.0 us)
Async XLA Ops:
  7.4 270.0 %all-reduce.4.cloned.1.call-start = ((), (), s32[]{:S(2)}) async-start(), calls=%async_computation.1 | async-start | bytes 4194304 | tf_op jit(solution)/shard_map/psum | solution.py:14
  11.1 1.3 copy-start
  11.1 2.8 copy-start.1
  11.1 294.7 %all-gather.2.cloned.1.call-start = ((), (), s32[]{:S(2)}) async-start(), calls=%async_computation.2 | async-start | bytes 10485760 | tf_op jit(solution)/shard_map/all_gather | solution.py:62
Sparse Core Ops, SparseCore 0:
  11.2 266.1 all-reduce.3
Sparse Core Ops, SparseCore 1:
  13.7 95.2 all-gather.1
where the time goes:
time: 445 us; the launch traced here: 444 us
  waiting for transfers between devices  264 us (59%)
  blocking collectives  107 us (24%)
  matrix products  30.9 us (7%)
  local copies, waits for them, and re-layouts  17.1 us (4%)
  between operations  16.3 us (4%)
  other arithmetic  8.64 us (2%)
    psum x1, waiting for transfers between devices, spread(): return lax.psum(kept, axis)  264 us
    unnamed x1, blocking collectives  78.4 us
    all_to_all x1, blocking collectives, body(): lax.all_to_all(summed.reshape(1, row_count, prompt_count, col_count), 'pr...  28.7 us
    dot_general x1, local copies, waits for them, and re-layouts, body(): jnp.dot(outputs, lax.all_gather(out_weight, 'prompt', axis=1, tiled=True)...  12 us
    dot_general x4, matrix products, head_block(): jnp.einsum('qd,kd->qk', query_block, key_rows, preferred_element_type=jnp...  11 us
    dot_general x1, matrix products, body(): jnp.dot(outputs, lax.all_gather(out_weight, 'prompt', axis=1, tiled=True)...  10.5 us
    dot_general x4, matrix products, head_block(): jnp.dot(weights, value_rows, preferred_element_type=jnp.float32)  9.42 us
  transfers between devices with their start and end apart: 2, of which 1 were waited for; matrix products, arithmetic and copies ran while one was open for 7% of the time, Pallas kernels for 0%

commit v1 on v0

v1 whole, which is shorter than its diff:
```python
import math

import jax
import jax.numpy as jnp
from jax import lax
from jax.experimental import pallas as pl
from jax.experimental.pallas import tpu as pltpu
from jax.sharding import PartitionSpec as P

HD = 128
SUF = 256
NX = 4
NZ = 4
GROUP = 8
EXP2_SCALE = math.log2(math.e) / math.sqrt(HD)
MASKED = -1e30


def cand_pairs(f):
    pairs = []
    for x in range(NX):
        for z in range(NZ):
            tx, tz = f(x, z)
            pairs.append((x * NZ + z, (tx % NX) * NZ + tz))
    return pairs


def ring_pairs(n, shift):
    return [(i, (i + shift) % n) for i in range(n)]


SCATTER_GROUPS = [
    [x * NZ + 2 * pair + zi for zi in range(2) for x in range(NX)] for pair in range(2)
]


def dot_t(a, b):
    return lax.dot_general(a, b, (((1,), (1,)), ((), ())), preferred_element_type=jnp.float32)


def dot_n(a, b):
    return lax.dot_general(a, b, (((1,), (0,)), ((), ())), preferred_element_type=jnp.float32)


def with_ones(values):
    return jnp.concatenate([values, jnp.ones_like(values)], axis=1)


def attention_kernel(n_blocks, has_suffix, has_state, last, heads, scalar_ref, *refs):
    refs = list(refs)
    q_ref = refs.pop(0)
    block_refs = [(refs.pop(0), refs.pop(0)) for _ in range(n_blocks)]
    suffix_ref = refs.pop(0) if has_suffix else None
    state_refs = [refs.pop(0) for _ in range(3)] if has_state else None
    outs = refs
    rows = q_ref.shape[0]
    keys_first = scalar_ref[0] == 1
    keys = [jnp.where(keys_first, a[...], b[...]) for a, b in block_refs]
    values = [with_ones(jnp.where(keys_first, b[...], a[...])) for a, b in block_refs]
    if has_suffix:
        keys.append(suffix_ref[0])
        values.append(with_ones(suffix_ref[1]))
        row = lax.broadcasted_iota(jnp.int32, (rows, rows), 0)
        col = lax.broadcasted_iota(jnp.int32, (rows, rows), 1)
        allowed = (col <= row) & (col < scalar_ref[1])
    for h in range(heads):
        lanes = pl.ds(h * HD, HD)
        query = q_ref[:, lanes]
        scores = [dot_t(query, k) * EXP2_SCALE for k in keys]
        if has_suffix:
            scores[-1] = jnp.where(allowed, scores[-1], MASKED)
        row_max = scores[0].max(axis=1, keepdims=True)
        for s in scores[1:]:
            row_max = jnp.maximum(row_max, s.max(axis=1, keepdims=True))
        if has_state:
            old_max = state_refs[1][:, lanes]
            new_max = jnp.maximum(old_max, row_max)
            row_max = new_max[:, :1]
        total = None
        for s, v in zip(scores, values):
            weights = jnp.exp2(s - row_max).astype(jnp.bfloat16)
            part = dot_n(weights, v)
            total = part if total is None else total + part
        acc, denom = total[:, :HD], total[:, HD:]
        if has_state:
            alpha = jnp.exp2(old_max - new_max)
            acc = acc + alpha * state_refs[0][:, lanes]
            denom = denom + alpha * state_refs[2][:, lanes]
        if last:
            outs[0][:, lanes] = (acc / denom).astype(jnp.bfloat16)
        else:
            outs[0][:, lanes] = acc
            outs[1][:, lanes] = jnp.broadcast_to(row_max, (rows, HD))
            outs[2][:, lanes] = denom


def attend(scalars, query_rows, blocks, suffix=None, state=None, last=False):
    rows, width = query_rows.shape
    heads = width // HD
    operands = [query_rows]
    for block in blocks:
        operands.extend(block)
    key_count = sum(a.shape[0] for a, _ in blocks)
    if suffix is not None:
        operands.append(suffix)
        key_count += suffix.shape[1]
    if state is not None:
        operands.extend(state)
    vmem = pl.BlockSpec(memory_space=pltpu.VMEM)
    if last:
        out_shape = [jax.ShapeDtypeStruct((rows, width), jnp.bfloat16)]
    else:
        out_shape = [jax.ShapeDtypeStruct((rows, width), jnp.float32)] * 3
    out = pl.pallas_call(
        lambda *refs: attention_kernel(
            len(blocks), suffix is not None, state is not None, last, heads, *refs
        ),
        out_shape=out_shape,
        in_specs=[pl.BlockSpec(memory_space=pltpu.SMEM)] + [vmem] * len(operands),
        out_specs=[vmem] * len(out_shape),
        compiler_params=pltpu.CompilerParams(vmem_limit_bytes=40 * 1024 * 1024),
        cost_estimate=pl.CostEstimate(
            flops=8 * rows * heads * key_count * HD,
            bytes_accessed=2**22,
            transcendentals=rows * heads * key_count,
        ),
    )(scalars, *operands)
    return out[0] if last else out


def spread_piece(prompt_kv, owner):
    me = lax.axis_index("cand")
    z = me % NZ
    owner_x, owner_z = owner // NZ, owner % NZ
    pieces = prompt_kv.reshape(GROUP, -1, HD)
    arrived = lax.all_to_all(
        pieces, "cand", split_axis=0, concat_axis=0, axis_index_groups=SCATTER_GROUPS
    )
    piece = lax.dynamic_index_in_dim(
        arrived, (owner_z % 2) * NX + owner_x, axis=0, keepdims=False
    )
    crossed = lax.ppermute(piece, "cand", cand_pairs(lambda x, z: (x, z ^ 2)))
    return jnp.where(owner_z // 2 == z // 2, piece, crossed)


def projection_kernel(core_ref, rows_ref, own_ref, other_ref, out_ref):
    rows = rows_ref[...]
    core = core_ref[0]
    n = own_ref.shape[1] // HD
    for i in range(n):
        lanes = pl.ds(i * HD, HD)
        both = dot_n(rows, jnp.concatenate([own_ref[:, lanes], other_ref[:, lanes]], axis=1))
        both = both.astype(jnp.bfloat16)
        out_ref[core * n + i] = both[:, :HD]
        out_ref[(1 - core) * n + i] = both[:, HD:]


def project(rows, own, other):
    count, depth = rows.shape
    width = own.shape[1]
    core = (lax.axis_index("prompt") % 2).astype(jnp.int32).reshape(1)
    vmem = pl.BlockSpec(memory_space=pltpu.VMEM)
    return pl.pallas_call(
        projection_kernel,
        out_shape=jax.ShapeDtypeStruct((2 * width // HD, count, HD), jnp.bfloat16),
        in_specs=[pl.BlockSpec(memory_space=pltpu.SMEM)] + [vmem] * 3,
        out_specs=vmem,
        compiler_params=pltpu.CompilerParams(vmem_limit_bytes=32 * 1024 * 1024),
        cost_estimate=pl.CostEstimate(
            flops=80 * width * count * depth,
            bytes_accessed=4 * depth * width,
            transcendentals=0,
        ),
    )(core, rows, own, other)


def exchange(products):
    n = products.shape[0]
    return lax.all_to_all(
        products,
        ("prompt", "tensor"),
        split_axis=0,
        concat_axis=0,
        axis_index_groups=[list(range(n)), list(range(n, 2 * n))],
    )


def add_up(terms):
    n, rows, columns = terms.shape
    terms = terms.reshape(2, n // 2, rows, columns).astype(jnp.float32)
    return terms.sum(axis=1).astype(jnp.bfloat16)


def swap(value, bit):
    return lax.ppermute(value, "prompt", [(p, p ^ bit) for p in range(4)])


def move(value, shift):
    return lax.ppermute(value, "cand", cand_pairs(lambda x, z: (x + shift, z)))


def body(owner_index, suffix_lengths, queries, suffix_kv, prompt_cache, out_weight):
    query_rows = queries[0]
    weights = [out_weight, swap(out_weight, 1)]
    piece = spread_piece(prompt_cache[:, 0, 0], owner_index[0])
    keys_first = (lax.axis_index("cand") % 2 == 0).astype(jnp.int32)
    scalars = jnp.stack([keys_first, suffix_lengths[0, 0]])
    other = lax.ppermute(piece, "cand", cand_pairs(lambda x, z: (x, z ^ 1)))
    left, right = [move(piece, 1)], [move(piece, -1)]
    left.append(move(other, 1))
    right.append(move(other, -1))
    across = [move(right[0], -1), move(left[1], 1)]
    state = attend(scalars, query_rows, [(piece, other)], suffix=suffix_kv[:, 0])
    state = attend(scalars, query_rows, [left, right], state=state)
    attended = attend(scalars, query_rows, [across], state=state, last=True)
    far_rows = swap(attended, 2)
    near = add_up(exchange(project(attended, *weights)))
    far = add_up(exchange(project(far_rows, *weights)))
    first = lax.axis_index("prompt") < 2
    return jnp.concatenate([jnp.where(first, near, far), jnp.where(first, far, near)])


def solution(mesh):
    in_specs = (
        P("prompt"),
        P("prompt", "cand"),
        P("prompt", "cand", "tensor"),
        P(None, "prompt", "cand", "tensor"),
        P(None, "prompt", "cand", None, "tensor"),
        P("tensor", "prompt"),
    )
    out_specs = P(None, "cand", ("prompt", "tensor"))
    return jax.shard_map(body, mesh=mesh, in_specs=in_specs, out_specs=out_specs, check_vma=False)
```

time: 445 us -> 171 us (0.38)
  waiting for transfers between devices: 264 us -> 77.6 us
  blocking collectives: 107 us -> 0 us
  starting transfers between devices: 0.05 us -> 63.6 us
  matrix products: 30.9 us -> 0 us
  Pallas kernels: 0 us -> 23.2 us
  local copies, waits for them, and re-layouts: 17.1 us -> 0.98 us
  between operations: 16.3 us -> 1.63 us
  other arithmetic: 8.64 us -> 3.31 us
    psum x1 -> x0, waiting for transfers between devices: 264 us -> none  [spread(): return lax.psum(kept, axis)]
    unnamed x1 -> x0, blocking collectives: 78.4 us -> none
    all_to_all x0 -> x3, waiting for transfers between devices: none -> 66.1 us  [the longest x2 48.1 us: exchange(): lax.all_to_all(products, ('prompt', 'tensor'), split_axis=0, concat_axis=...]
    ppermute x0 -> x10, starting transfers between devices: none -> 41.7 us  [the longest x6 17.2 us: move(): return lax.ppermute(value, 'cand', cand_pairs(lambda x, z: (x + shift, z)))]
    dot_general x9 -> x0, matrix products: 30.9 us -> none  [the longest x4 11 us: head_block(): jnp.einsum('qd,kd->qk', query_block, key_rows, preferred_element_type=jnp...]
    all_to_all x1 -> x0, blocking collectives: 28.7 us -> none  [body(): lax.all_to_all(summed.reshape(1, row_count, prompt_count, col_count), 'pr...]
    pallas_call x0 -> x5, Pallas kernels: none -> 23.2 us  [the longest x3 15.4 us: attend(): pl.pallas_call(lambda *refs: attention_kernel(len(blocks), suffix is not...]
    all_to_all x0 -> x3, starting transfers between devices: none -> 21.9 us  [the longest x2 14.9 us: exchange(): lax.all_to_all(products, ('prompt', 'tensor'), split_axis=0, concat_axis=...]
  transfers between devices with their start and end apart: 2 -> 13, of which waited for: 1 -> 4; matrix products, arithmetic and copies ran while one was open for 7% -> 2% of each run, Pallas kernels for 0% -> 14%
where the time goes in v1:
time: 171 us; the launch traced here: 170 us
  waiting for transfers between devices  77.6 us (45%)
  starting transfers between devices  63.6 us (37%)
  Pallas kernels  23.2 us (14%)
  other arithmetic  3.31 us (2%)
    all_to_all x2, waiting for transfers between devices, exchange(): lax.all_to_all(products, ('prompt', 'tensor'), split_axis=0, concat_axis=...  48.1 us
    all_to_all x1, waiting for transfers between devices, spread_piece(): lax.all_to_all(pieces, 'cand', split_axis=0, concat_axis=0, axis_index_gr...  18 us
    ppermute x6, starting transfers between devices, move(): return lax.ppermute(value, 'cand', cand_pairs(lambda x, z: (x + shift, z)))  17.2 us
    pallas_call x3, Pallas kernels, attend(): pl.pallas_call(lambda *refs: attention_kernel(len(blocks), suffix is not...  15.4 us
    all_to_all x2, starting transfers between devices, exchange(): lax.all_to_all(products, ('prompt', 'tensor'), split_axis=0, concat_axis=...  14.9 us
    ppermute x2, starting transfers between devices, swap(): return lax.ppermute(value, 'prompt', [(p, p ^ bit) for p in range(4)])  14.4 us
    ppermute x1, waiting for transfers between devices, spread_piece(): crossed = lax.ppermute(piece, 'cand', cand_pairs(lambda x, z: (x, z ^ 2)))  11.4 us
    pallas_call x2, Pallas kernels, project(): pl.pallas_call(projection_kernel, out_shape=jax.ShapeDtypeStruct((2 * wid...  7.79 us
  transfers between devices with their start and end apart: 13, of which 4 were waited for; matrix products, arithmetic and copies ran while one was open for 2% of the time, Pallas kernels for 14%

profile of v1, /device:TPU:1, one launch (start us, length us, event | category | flops | bytes accessed | tf_op | source)
XLA Modules:
  0.0 170.2 jit_solution(14222052622894921818)
XLA Ops:
  0.0 6.9 %all-to-all-start = ((bf16[8,1024,128]{2,1,0:T(8,128)(2,1)}), bf16[8,1024,128]{2,1,0:T(8,128)(2,1)}, u32[]{:S(2)}, u32[]{:S(2)}) async-start(bf16[8,1024,128]{2,1,0:T(8,128)(2,1)} %bitcast.24), calls=%async_computation | async-start | bytes 4194304 | tf_op jit(solution)/shard_map/all_to_all | solution.py:136
  6.9 6.5 %collective-permute-start.8 = (bf16[1024,1024]{1,0:T(8,128)(2,1)S(1)}, bf16[1024,1024]{1,0:T(8,128)(2,1)}, u32[]{:S(2)}, u32[]{:S(2)}) collective-permute-start(bf16[1024,1024]{1,0:T(8,128)(2,1)S(1)} %copy-done), channel_id=1, source_target_pairs={{0,8},{8,0},{16,24},{24,16},{1,9},{9,1},{17,25},{25,17},{2,10},{10... | collective-permute-start | bytes 6291464 | tf_op jit(solution)/shard_map/ppermute | solution.py:195
  14.1 18.0 %all-to-all-done = bf16[8,1024,128]{2,1,0:T(8,128)(2,1)} async-done(((bf16[8,1024,128]{2,1,0:T(8,128)(2,1)}), bf16[8,1024,128]{2,1,0:T(8,128)(2,1)}, u32[]{:S(2)}, u32[]{:S(2)}) %all-to-all-start) | async-done | bytes 2097184 | tf_op jit(solution)/shard_map/all_to_all | solution.py:136
  32.2 1.0 dynamic-slice_bitcast_fusion
  33.2 6.8 %collective-permute-start = (bf16[1024,128]{1,0:T(8,128)(2,1)S(1)}, bf16[1024,128]{1,0:T(8,128)(2,1)S(1)}, u32[]{:S(2)}, u32[]{:S(2)}) collective-permute-start(bf16[1024,128]{1,0:T(8,128)(2,1)S(1)} %dynamic-slice_bitcast_fusion), channel_id=1, source_target_pairs={{0,64},{32,96},{64,0},{96,32},{128,192},{160,224},{192,128},{224,1... | collective-permute-start | bytes 786440 | tf_op jit(solution)/shard_map/ppermute | solution.py:142
  40.0 11.4 %collective-permute-done = bf16[1024,128]{1,0:T(8,128)(2,1)S(1)} collective-permute-done((bf16[1024,128]{1,0:T(8,128)(2,1)S(1)}, bf16[1024,128]{1,0:T(8,128)(2,1)S(1)}, u32[]{:S(2)}, u32[]{:S(2)}) %collective-permute-start) | collective-permute-done | bytes 262176 | tf_op jit(solution)/shard_map/ppermute | solution.py:142
  51.4 1.0 broadcast_select_fusion.refs_2_
  52.4 3.2 %collective-permute-start.3 = (bf16[1024,128]{1,0:T(8,128)(2,1)S(1)}, bf16[1024,128]{1,0:T(8,128)(2,1)S(1)}, u32[]{:S(2)}, u32[]{:S(2)}) collective-permute-start(bf16[1024,128]{1,0:T(8,128)(2,1)S(1)} %broadcast_select_fusion.refs_2_), channel_id=1, source_target_pairs={{0,32},{32,0},{64,96},{96,64},{128,160},{160,128},{192,224},{224,1... | collective-permute-start | bytes 786440 | tf_op jit(solution)/shard_map/ppermute | solution.py:208
  55.7 2.6 %collective-permute-start.1 = (bf16[1024,128]{1,0:T(8,128)(2,1)S(1)}, bf16[1024,128]{1,0:T(8,128)(2,1)S(1)}, u32[]{:S(2)}, u32[]{:S(2)}) collective-permute-start(bf16[1024,128]{1,0:T(8,128)(2,1)S(1)} %broadcast_select_fusion.refs_2_), channel_id=1, source_target_pairs={{0,384},{32,416},{64,448},{96,480},{128,0},{160,32},{192,64},{224,... | collective-permute-start | bytes 786440 | tf_op jit(solution)/shard_map/ppermute | solution.py:199
  58.9 2.7 %collective-permute-start.6 = (bf16[1024,128]{1,0:T(8,128)(2,1)S(1)}, bf16[1024,128]{1,0:T(8,128)(2,1)}, u32[]{:S(2)}, u32[]{:S(2)}) collective-permute-start(bf16[1024,128]{1,0:T(8,128)(2,1)S(1)} %broadcast_select_fusion.refs_2_), channel_id=1, source_target_pairs={{0,128},{32,160},{64,192},{96,224},{128,256},{160,288},{192,320},{... | collective-permute-start | bytes 786440 | tf_op jit(solution)/shard_map/ppermute | solution.py:199
  61.6 0.0 collective-permute-done.3.refs_3_
  61.7 1.9 %collective-permute-start.4 = (bf16[1024,128]{1,0:T(8,128)(2,1)S(1)}, bf16[1024,128]{1,0:T(8,128)(2,1)}, u32[]{:S(2)}, u32[]{:S(2)}) collective-permute-start(bf16[1024,128]{1,0:T(8,128)(2,1)S(1)} %collective-permute-done.3.refs_3_), channel_id=1, source_target_pairs={{0,128},{32,160},{64,192},{96,224},{128,256},{160,288},{192,320},{... | collective-permute-start | bytes 786440 | tf_op jit(solution)/shard_map/ppermute | solution.py:199
  63.6 4.6 %collective-permute-start.7 = (bf16[1024,128]{1,0:T(8,128)(2,1)S(1)}, bf16[1024,128]{1,0:T(8,128)(2,1)}, u32[]{:S(2)}, u32[]{:S(2)}) collective-permute-start(bf16[1024,128]{1,0:T(8,128)(2,1)S(1)} %collective-permute-done.3.refs_3_), channel_id=1, source_target_pairs={{0,384},{32,416},{64,448},{96,480},{128,0},{160,32},{192,64},{224,... | collective-permute-start | bytes 786440 | tf_op jit(solution)/shard_map/ppermute | solution.py:199
  68.2 0.1 pad_add_fusion.refs_0_
  68.2 0.0 collective-permute-done.1.refs_4_
  68.2 2.5 %collective-permute-start.2 = (bf16[1024,128]{1,0:T(8,128)(2,1)S(1)}, bf16[1024,128]{1,0:T(8,128)(2,1)S(1)}, u32[]{:S(2)}, u32[]{:S(2)}) collective-permute-start(bf16[1024,128]{1,0:T(8,128)(2,1)S(1)} %collective-permute-done.1.refs_4_), channel_id=1, source_target_pairs={{0,384},{32,416},{64,448},{96,480},{128,0},{160,32},{192,64},{224,... | collective-permute-start | bytes 786440 | tf_op jit(solution)/shard_map/ppermute | solution.py:199
  70.8 4.3 %shard_map.64 = (f32[256,1024]{1,0:T(8,128)S(1)}, f32[256,1024]{1,0:T(8,128)S(1)}, f32[256,1024]{1,0:T(8,128)S(1)}) custom-call(s32[2]{0:T(128)S(1)} %pad_add_fusion.refs_0_, bf16[256,1024]{1,0:T(8,128)(2,1)S(1)} %bitcast.20, bf16[1024,128]{1,0:T(8,128)(2,1)S(1)} %broadcast_select_fusion.refs_2_, bf16[1024,128]{1,0:T(8,128)(2,1)S(1)} %collective-permute-done.3.refs_3_, ...), custom_call_target="tpu_custom_call" | custom-call | flops 2684354560 | bytes 4194304 | tf_op jit(solution)/shard_map/pallas_call | solution.py:114
  75.1 2.9 %collective-permute-start.5 = (bf16[1024,128]{1,0:T(8,128)(2,1)}, bf16[1024,128]{1,0:T(8,128)(2,1)S(1)}, u32[]{:S(2)}, u32[]{:S(2)}) collective-permute-start(bf16[1024,128]{1,0:T(8,128)(2,1)} %collective-permute-done.4.refs_3_), channel_id=1, source_target_pairs={{0,128},{32,160},{64,192},{96,224},{128,256},{160,288},{192,320},{... | collective-permute-start | bytes 786440 | tf_op jit(solution)/shard_map/ppermute | solution.py:199
  78.0 0.0 collective-permute-done.6.refs_2_
  78.0 7.2 %shard_map.65 = (f32[256,1024]{1,0:T(8,128)S(1)}, f32[256,1024]{1,0:T(8,128)S(1)}, f32[256,1024]{1,0:T(8,128)S(1)}) custom-call(s32[2]{0:T(128)S(1)} %pad_add_fusion.refs_0_, bf16[256,1024]{1,0:T(8,128)(2,1)S(1)} %bitcast.21, bf16[1024,128]{1,0:T(8,128)(2,1)} %collective-permute-done.6.refs_2_, bf16[1024,128]{1,0:T(8,128)(2,1)} %collective-permute-done.4.refs_3_, ...), custom_call_target="tpu_custom_call" | custom-call | flops 4294967296 | bytes 4194304 | tf_op jit(solution)/shard_map/pallas_call | solution.py:114
  85.2 0.0 collective-permute-done.5.refs_3_
  85.3 3.9 %shard_map.66.rows_ref = bf16[256,1024]{1,0:T(8,128)(2,1)S(1)} custom-call(s32[2]{0:T(128)S(1)} %pad_add_fusion.refs_0_, bf16[256,1024]{1,0:T(8,128)(2,1)S(1)} %bitcast.22, bf16[1024,128]{1,0:T(8,128)(2,1)S(1)} %collective-permute-done.2.refs_2_, bf16[1024,128]{1,0:T(8,128)(2,1)S(1)} %collective-permute-done.5.refs_3_, ...), custom_call_target="tpu_custom_call" | custom-call | flops 2147483648 | bytes 4194304 | tf_op jit(solution)/shard_map/pallas_call | solution.py:114
  89.2 7.9 %collective-permute-start.9 = (bf16[256,1024]{1,0:T(8,128)(2,1)S(1)}, bf16[256,1024]{1,0:T(8,128)(2,1)S(1)}, u32[]{:S(2)}, u32[]{:S(2)}) collective-permute-start(bf16[256,1024]{1,0:T(8,128)(2,1)S(1)} %shard_map.66.rows_ref), channel_id=1, source_target_pairs={{0,16},{8,24},{16,0},{24,8},{1,17},{9,25},{17,1},{25,9},{2,18},{10... | collective-permute-start | bytes 1572872 | tf_op jit(solution)/shard_map/ppermute | solution.py:195
  97.1 3.9 %shard_map.67 = bf16[16,256,128]{2,1,0:T(8,128)(2,1)} custom-call(s32[1]{0:T(128)} %bitcast.core_ref, bf16[256,1024]{1,0:T(8,128)(2,1)S(1)} %shard_map.66.rows_ref, bf16[1024,1024]{1,0:T(8,128)(2,1)S(1)} %copy-done, bf16[1024,1024]{1,0:T(8,128)(2,1)} %collective-permute-done.8.other_ref), custom_call_target="tpu_custom_call" | custom-call | flops 21474836480 | bytes 4194304 | tf_op jit(solution)/shard_map/pallas_call | solution.py:163
  101.0 10.1 %all-to-all-start.1 = ((bf16[16,256,128]{2,1,0:T(8,128)(2,1)}), bf16[16,256,128]{2,1,0:T(8,128)(2,1)}, u32[]{:S(2)}, u32[]{:S(2)}) async-start(bf16[16,256,128]{2,1,0:T(8,128)(2,1)} %shard_map.67), calls=%async_computation.1 | async-start | bytes 2097152 | tf_op jit(solution)/shard_map/all_to_all | solution.py:179
  111.2 3.9 %shard_map.68 = bf16[16,256,128]{2,1,0:T(8,128)(2,1)} custom-call(s32[1]{0:T(128)} %bitcast.core_ref, bf16[256,1024]{1,0:T(8,128)(2,1)S(1)} %collective-permute-done.9.rows_ref, bf16[1024,1024]{1,0:T(8,128)(2,1)S(1)} %copy-done, bf16[1024,1024]{1,0:T(8,128)(2,1)} %collective-permute-done.8.other_ref), custom_call_target="tpu_custom_call" | custom-call | flops 21474836480 | bytes 4194304 | tf_op jit(solution)/shard_map/pallas_call | solution.py:163
  115.0 22.8 %all-to-all-done.1 = bf16[16,256,128]{2,1,0:T(8,128)(2,1)} async-done(((bf16[16,256,128]{2,1,0:T(8,128)(2,1)}), bf16[16,256,128]{2,1,0:T(8,128)(2,1)}, u32[]{:S(2)}, u32[]{:S(2)}) %all-to-all-start.1) | async-done | bytes 1048608 | tf_op jit(solution)/shard_map/all_to_all | solution.py:179
  137.9 4.8 %all-to-all-start.2 = ((bf16[16,256,128]{2,1,0:T(8,128)(2,1)}), bf16[16,256,128]{2,1,0:T(8,128)(2,1)S(1)}, u32[]{:S(2)}, u32[]{:S(2)}) async-start(bf16[16,256,128]{2,1,0:T(8,128)(2,1)} %shard_map.68), calls=%async_computation.2 | async-start | bytes 2097152 | tf_op jit(solution)/shard_map/all_to_all | solution.py:179
  142.7 1.4 bitcast_reduce_fusion.1
  144.1 25.3 %all-to-all-done.2 = bf16[16,256,128]{2,1,0:T(8,128)(2,1)S(1)} async-done(((bf16[16,256,128]{2,1,0:T(8,128)(2,1)}), bf16[16,256,128]{2,1,0:T(8,128)(2,1)S(1)}, u32[]{:S(2)}, u32[]{:S(2)}) %all-to-all-start.2) | async-done | bytes 1048608 | tf_op jit(solution)/shard_map/all_to_all | solution.py:179
  169.3 0.1 bitcast_reduce_fusion
  169.5 0.7 pad_maximum_fusion
  (12 shorter events, 0.0 us)
Async XLA Ops:
  0.0 6.9 %copy-start = (bf16[1024,1024]{1,0:T(8,128)(2,1)S(1)}, bf16[1024,1024]{1,0:T(8,128)(2,1)}, u32[]{:S(2)}) copy-start(bf16[1024,1024]{1,0:T(8,128)(2,1)} %own_ref.3) | copy-start | bytes 6291460
  0.0 70.8 %copy-start.1 = (bf16[1,256,1024]{2,1,0:T(8,128)(2,1)S(1)}, bf16[1,256,1024]{2,1,0:T(8,128)(2,1)}, u32[]{:S(2)}) copy-start(bf16[1,256,1024]{2,1,0:T(8,128)(2,1)} %param.8) | copy-start | bytes 1572868
  0.0 70.8 %copy-start.2 = (bf16[2,1,256,128]{3,2,1,0:T(8,128)(2,1)S(1)}, bf16[2,1,256,128]{3,2,1,0:T(8,128)(2,1)}, u32[]{:S(2)}) copy-start(bf16[2,1,256,128]{3,2,1,0:T(8,128)(2,1)} %param.9) | copy-start | bytes 393220
  0.0 32.2 %all-to-all-start = ((bf16[8,1024,128]{2,1,0:T(8,128)(2,1)}), bf16[8,1024,128]{2,1,0:T(8,128)(2,1)}, u32[]{:S(2)}, u32[]{:S(2)}) async-start(bf16[8,1024,128]{2,1,0:T(8,128)(2,1)} %bitcast.24), calls=%async_computation | async-start | bytes 4194304 | tf_op jit(solution)/shard_map/all_to_all | solution.py:136
  6.9 90.2 %collective-permute-start.8 = (bf16[1024,1024]{1,0:T(8,128)(2,1)S(1)}, bf16[1024,1024]{1,0:T(8,128)(2,1)}, u32[]{:S(2)}, u32[]{:S(2)}) collective-permute-start(bf16[1024,1024]{1,0:T(8,128)(2,1)S(1)} %copy-done), channel_id=1, source_target_pairs={{0,8},{8,0},{16,24},{24,16},{1,9},{9,1},{17,25},{25,17},{2,10},{10... | collective-permute-start | bytes 6291464 | tf_op jit(solution)/shard_map/ppermute | solution.py:195
  33.2 18.3 %collective-permute-start = (bf16[1024,128]{1,0:T(8,128)(2,1)S(1)}, bf16[1024,128]{1,0:T(8,128)(2,1)S(1)}, u32[]{:S(2)}, u32[]{:S(2)}) collective-permute-start(bf16[1024,128]{1,0:T(8,128)(2,1)S(1)} %dynamic-slice_bitcast_fusion), channel_id=1, source_target_pairs={{0,64},{32,96},{64,0},{96,32},{128,192},{160,224},{192,128},{224,1... | collective-permute-start | bytes 786440 | tf_op jit(solution)/shard_map/ppermute | solution.py:142
  52.4 9.2 %collective-permute-start.3 = (bf16[1024,128]{1,0:T(8,128)(2,1)S(1)}, bf16[1024,128]{1,0:T(8,128)(2,1)S(1)}, u32[]{:S(2)}, u32[]{:S(2)}) collective-permute-start(bf16[1024,128]{1,0:T(8,128)(2,1)S(1)} %broadcast_select_fusion.refs_2_), channel_id=1, source_target_pairs={{0,32},{32,0},{64,96},{96,64},{128,160},{160,128},{192,224},{224,1... | collective-permute-start | bytes 786440 | tf_op jit(solution)/shard_map/ppermute | solution.py:208
  55.7 12.6 %collective-permute-start.1 = (bf16[1024,128]{1,0:T(8,128)(2,1)S(1)}, bf16[1024,128]{1,0:T(8,128)(2,1)S(1)}, u32[]{:S(2)}, u32[]{:S(2)}) collective-permute-start(bf16[1024,128]{1,0:T(8,128)(2,1)S(1)} %broadcast_select_fusion.refs_2_), channel_id=1, source_target_pairs={{0,384},{32,416},{64,448},{96,480},{128,0},{160,32},{192,64},{224,... | collective-permute-start | bytes 786440 | tf_op jit(solution)/shard_map/ppermute | solution.py:199
  58.9 19.1 %collective-permute-start.6 = (bf16[1024,128]{1,0:T(8,128)(2,1)S(1)}, bf16[1024,128]{1,0:T(8,128)(2,1)}, u32[]{:S(2)}, u32[]{:S(2)}) collective-permute-start(bf16[1024,128]{1,0:T(8,128)(2,1)S(1)} %broadcast_select_fusion.refs_2_), channel_id=1, source_target_pairs={{0,128},{32,160},{64,192},{96,224},{128,256},{160,288},{192,320},{... | collective-permute-start | bytes 786440 | tf_op jit(solution)/shard_map/ppermute | solution.py:199
  61.7 13.4 %collective-permute-start.4 = (bf16[1024,128]{1,0:T(8,128)(2,1)S(1)}, bf16[1024,128]{1,0:T(8,128)(2,1)}, u32[]{:S(2)}, u32[]{:S(2)}) collective-permute-start(bf16[1024,128]{1,0:T(8,128)(2,1)S(1)} %collective-permute-done.3.refs_3_), channel_id=1, source_target_pairs={{0,128},{32,160},{64,192},{96,224},{128,256},{160,288},{192,320},{... | collective-permute-start | bytes 786440 | tf_op jit(solution)/shard_map/ppermute | solution.py:199
  63.6 14.4 %collective-permute-start.7 = (bf16[1024,128]{1,0:T(8,128)(2,1)S(1)}, bf16[1024,128]{1,0:T(8,128)(2,1)}, u32[]{:S(2)}, u32[]{:S(2)}) collective-permute-start(bf16[1024,128]{1,0:T(8,128)(2,1)S(1)} %collective-permute-done.3.refs_3_), channel_id=1, source_target_pairs={{0,384},{32,416},{64,448},{96,480},{128,0},{160,32},{192,64},{224,... | collective-permute-start | bytes 786440 | tf_op jit(solution)/shard_map/ppermute | solution.py:199
  68.2 17.0 %collective-permute-start.2 = (bf16[1024,128]{1,0:T(8,128)(2,1)S(1)}, bf16[1024,128]{1,0:T(8,128)(2,1)S(1)}, u32[]{:S(2)}, u32[]{:S(2)}) collective-permute-start(bf16[1024,128]{1,0:T(8,128)(2,1)S(1)} %collective-permute-done.1.refs_4_), channel_id=1, source_target_pairs={{0,384},{32,416},{64,448},{96,480},{128,0},{160,32},{192,64},{224,... | collective-permute-start | bytes 786440 | tf_op jit(solution)/shard_map/ppermute | solution.py:199
  75.1 10.1 %collective-permute-start.5 = (bf16[1024,128]{1,0:T(8,128)(2,1)}, bf16[1024,128]{1,0:T(8,128)(2,1)S(1)}, u32[]{:S(2)}, u32[]{:S(2)}) collective-permute-start(bf16[1024,128]{1,0:T(8,128)(2,1)} %collective-permute-done.4.refs_3_), channel_id=1, source_target_pairs={{0,128},{32,160},{64,192},{96,224},{128,256},{160,288},{192,320},{... | collective-permute-start | bytes 786440 | tf_op jit(solution)/shard_map/ppermute | solution.py:199
  89.2 22.0 %collective-permute-start.9 = (bf16[256,1024]{1,0:T(8,128)(2,1)S(1)}, bf16[256,1024]{1,0:T(8,128)(2,1)S(1)}, u32[]{:S(2)}, u32[]{:S(2)}) collective-permute-start(bf16[256,1024]{1,0:T(8,128)(2,1)S(1)} %shard_map.66.rows_ref), channel_id=1, source_target_pairs={{0,16},{8,24},{16,0},{24,8},{1,17},{9,25},{17,1},{25,9},{2,18},{10... | collective-permute-start | bytes 1572872 | tf_op jit(solution)/shard_map/ppermute | solution.py:195
  101.0 36.8 %all-to-all-start.1 = ((bf16[16,256,128]{2,1,0:T(8,128)(2,1)}), bf16[16,256,128]{2,1,0:T(8,128)(2,1)}, u32[]{:S(2)}, u32[]{:S(2)}) async-start(bf16[16,256,128]{2,1,0:T(8,128)(2,1)} %shard_map.67), calls=%async_computation.1 | async-start | bytes 2097152 | tf_op jit(solution)/shard_map/all_to_all | solution.py:179
  137.9 31.5 %all-to-all-start.2 = ((bf16[16,256,128]{2,1,0:T(8,128)(2,1)}), bf16[16,256,128]{2,1,0:T(8,128)(2,1)S(1)}, u32[]{:S(2)}, u32[]{:S(2)}) async-start(bf16[16,256,128]{2,1,0:T(8,128)(2,1)} %shard_map.68), calls=%async_computation.2 | async-start | bytes 2097152 | tf_op jit(solution)/shard_map/all_to_all | solution.py:179

commit v2 on v1

--- a/solution.py
+++ b/solution.py
@@ -12,6 +12,7 @@
 NX = 4
 NZ = 4
 GROUP = 8
+CHUNK = 512
 EXP2_SCALE = math.log2(math.e) / math.sqrt(HD)
 MASKED = -1e30
 
@@ -55,20 +56,27 @@
     outs = refs
     rows = q_ref.shape[0]
     keys_first = scalar_ref[0] == 1
-    keys = [jnp.where(keys_first, a[...], b[...]) for a, b in block_refs]
-    values = [with_ones(jnp.where(keys_first, b[...], a[...])) for a, b in block_refs]
+    keys, values = [], []
+    for a, b in block_refs:
+        for start in range(0, a.shape[0], CHUNK):
+            chunk = pl.ds(start, CHUNK)
+            keys.append(jnp.where(keys_first, a[chunk], b[chunk]))
+            values.append(with_ones(jnp.where(keys_first, b[chunk], a[chunk])))
     if has_suffix:
         keys.append(suffix_ref[0])
         values.append(with_ones(suffix_ref[1]))
         row = lax.broadcasted_iota(jnp.int32, (rows, rows), 0)
         col = lax.broadcasted_iota(jnp.int32, (rows, rows), 1)
         allowed = (col <= row) & (col < scalar_ref[1])
-    for h in range(heads):
-        lanes = pl.ds(h * HD, HD)
+
+    def score(lanes):
         query = q_ref[:, lanes]
         scores = [dot_t(query, k) * EXP2_SCALE for k in keys]
         if has_suffix:
             scores[-1] = jnp.where(allowed, scores[-1], MASKED)
+        return lanes, scores
+
+    def weigh(lanes, scores):
         row_max = scores[0].max(axis=1, keepdims=True)
         for s in scores[1:]:
             row_max = jnp.maximum(row_max, s.max(axis=1, keepdims=True))
@@ -92,6 +100,14 @@
             outs[0][:, lanes] = acc
             outs[1][:, lanes] = jnp.broadcast_to(row_max, (rows, HD))
             outs[2][:, lanes] = denom
+
+    pending = None
+    for h in range(heads):
+        scored = score(pl.ds(h * HD, HD))
+        if pending is not None:
+            weigh(*pending)
+        pending = scored
+    weigh(*pending)
 
 
 def attend(scalars, query_rows, blocks, suffix=None, state=None, last=False):
@@ -143,51 +159,72 @@
     return jnp.where(owner_z // 2 == z // 2, piece, crossed)
 
 
-def projection_kernel(core_ref, rows_ref, own_ref, other_ref, out_ref):
+def projection_kernel(kept, place_ref, own_ref, other_ref, rows_ref, *out_refs):
     rows = rows_ref[...]
-    core = core_ref[0]
-    n = own_ref.shape[1] // HD
-    for i in range(n):
-        lanes = pl.ds(i * HD, HD)
+    core, parity = place_ref[0], place_ref[1]
+    for j in range(own_ref.shape[1] // HD // 2):
+        block = 2 * j + (parity if kept else 1 - parity)
+        lanes = pl.ds(pl.multiple_of(block * HD, HD), HD)
         both = dot_n(rows, jnp.concatenate([own_ref[:, lanes], other_ref[:, lanes]], axis=1))
-        both = both.astype(jnp.bfloat16)
-        out_ref[core * n + i] = both[:, :HD]
-        out_ref[(1 - core) * n + i] = both[:, HD:]
-
-
-def project(rows, own, other):
+        if kept:
+            out_refs[0][core, j] = both[:, :HD]
+            out_refs[0][1 - core, j] = both[:, HD:]
+        else:
+            out_refs[0][j] = both[:, :HD].astype(jnp.bfloat16)
+            out_refs[1][j] = both[:, HD:].astype(jnp.bfloat16)
+
+
+def project(rows, own, other, kept):
+    n = lax.axis_size("tensor") // 2
     count, depth = rows.shape
-    width = own.shape[1]
-    core = (lax.axis_index("prompt") % 2).astype(jnp.int32).reshape(1)
+    place = jnp.stack([lax.axis_index("prompt") % 2, lax.axis_index("tensor") % 2])
     vmem = pl.BlockSpec(memory_space=pltpu.VMEM)
+    if kept:
+        out_shape = [jax.ShapeDtypeStruct((2, n, count, HD), jnp.float32)]
+    else:
+        out_shape = [jax.ShapeDtypeStruct((n, count, HD), jnp.bfloat16)] * 2
     return pl.pallas_call(
-        projection_kernel,
-        out_shape=jax.ShapeDtypeStruct((2 * width // HD, count, HD), jnp.bfloat16),
+        lambda *refs: projection_kernel(kept, *refs),
+        out_shape=out_shape,
         in_specs=[pl.BlockSpec(memory_space=pltpu.SMEM)] + [vmem] * 3,
-        out_specs=vmem,
+        out_specs=[vmem] * len(out_shape),
         compiler_params=pltpu.CompilerParams(vmem_limit_bytes=32 * 1024 * 1024),
         cost_estimate=pl.CostEstimate(
-            flops=80 * width * count * depth,
-            bytes_accessed=4 * depth * width,
+            flops=80 * own.shape[1] * count * depth,
+            bytes_accessed=4 * own.size,
             transcendentals=0,
         ),
-    )(core, rows, own, other)
-
-
-def exchange(products):
-    n = products.shape[0]
-    return lax.all_to_all(
-        products,
+    )(place.astype(jnp.int32), own, other, rows)
+
+
+def pair_sums(rows, own, other):
+    own_sent, other_sent = project(rows, own, other, kept=False)
+    n = lax.axis_size("tensor")
+    up = [(t, (t + 1) % n if t % 2 == 0 else t - 1) for t in range(n)]
+    down = [(t, (t - 1) % n if t % 2 == 0 else (t + 1) % n) for t in range(n)]
+    own_got = lax.ppermute(own_sent, "tensor", up)
+    other_got = lax.ppermute(other_sent, "tensor", down)
+    (keep,) = project(rows, own, other, kept=True)
+    even = lax.axis_index("prompt") % 2 == 0
+    got = [jnp.where(even, own_got, other_got), jnp.where(even, other_got, own_got)]
+    return keep + jnp.stack(got).astype(jnp.float32)
+
+
+def exchange(terms):
+    cores, n, rows, columns = terms.shape
+    groups = [
+        [(2 * z + core) * 2 * n + 2 * j + parity for core in range(cores) for j in range(n)]
+        for z in range(2)
+        for parity in range(2)
+    ]
+    terms = lax.all_to_all(
+        terms.astype(jnp.bfloat16).reshape(cores * n, rows, columns),
         ("prompt", "tensor"),
         split_axis=0,
         concat_axis=0,
-        axis_index_groups=[list(range(n)), list(range(n, 2 * n))],
-    )
-
-
-def add_up(terms):
-    n, rows, columns = terms.shape
-    terms = terms.reshape(2, n // 2, rows, columns).astype(jnp.float32)
+        axis_index_groups=groups,
+    )
+    terms = terms.reshape(cores, n, rows, columns).astype(jnp.float32)
     return terms.sum(axis=1).astype(jnp.bfloat16)
 
 
@@ -214,8 +251,11 @@
     state = attend(scalars, query_rows, [left, right], state=state)
     attended = attend(scalars, query_rows, [across], state=state, last=True)
     far_rows = swap(attended, 2)
-    near = add_up(exchange(project(attended, *weights)))
-    far = add_up(exchange(project(far_rows, *weights)))
+    near_terms = pair_sums(attended, *weights)
+    near = exchange(near_terms)
+    _, far_rows = lax.optimization_barrier((near_terms, far_rows))
+    far_terms, _ = lax.optimization_barrier((pair_sums(far_rows, *weights), near))
+    far = exchange(far_terms)
     first = lax.axis_index("prompt") < 2
     return jnp.concatenate([jnp.where(first, near, far), jnp.where(first, far, near)])
 

time: 171 us -> 165 us (0.965)
  waiting for transfers between devices: 77.6 us -> 54.7 us
  starting transfers between devices: 63.6 us -> 76.7 us
    all_to_all x2, waiting for transfers between devices: 48.1 us -> 14.3 us  [exchange(): lax.all_to_all(terms.astype(jnp.bfloat16).reshape(cores * n, rows, column...]
    ppermute x0 -> x4, starting transfers between devices: none -> 14.6 us  [the longest x2 10.1 us: pair_sums(): other_got = lax.ppermute(other_sent, 'tensor', down)]
    ppermute x0 -> x4, waiting for transfers between devices: none -> 10.9 us  [the longest x2 8.88 us: pair_sums(): own_got = lax.ppermute(own_sent, 'tensor', up)]
    pallas_call x2 -> x4, Pallas kernels: 7.79 us -> 10.1 us  [project(): pl.pallas_call(lambda *refs: projection_kernel(kept, *refs), out_shape=ou...]
    add x0 -> x2, other arithmetic: none -> 1.82 us  [pair_sums(): return keep + jnp.stack(got).astype(jnp.float32)]
    pallas_call x3, Pallas kernels: 15.4 us -> 13.6 us  [attend(): pl.pallas_call(lambda *refs: attention_kernel(len(blocks), suffix is not...]
  transfers between devices with their start and end apart: 13 -> 17, of which waited for: 4 -> 6; matrix products, arithmetic and copies ran while one was open for 2% -> 2% of each run, Pallas kernels for 14% -> 15%
where the time goes in v2:
time: 165 us; the launch traced here: 163 us
  starting transfers between devices  76.7 us (46%)
  waiting for transfers between devices  54.7 us (33%)
  Pallas kernels  23.7 us (14%)
  other arithmetic  4.96 us (3%)
  between operations  1.73 us (1%)
    all_to_all x1, waiting for transfers between devices, spread_piece(): lax.all_to_all(pieces, 'cand', split_axis=0, concat_axis=0, axis_index_gr...  18.1 us
    ppermute x6, starting transfers between devices, move(): return lax.ppermute(value, 'cand', cand_pairs(lambda x, z: (x + shift, z)))  17.2 us
    ppermute x2, starting transfers between devices, swap(): return lax.ppermute(value, 'prompt', [(p, p ^ bit) for p in range(4)])  14.4 us
    all_to_all x2, waiting for transfers between devices, exchange(): lax.all_to_all(terms.astype(jnp.bfloat16).reshape(cores * n, rows, column...  14.3 us
    pallas_call x3, Pallas kernels, attend(): pl.pallas_call(lambda *refs: attention_kernel(len(blocks), suffix is not...  13.6 us
    all_to_all x2, starting transfers between devices, exchange(): lax.all_to_all(terms.astype(jnp.bfloat16).reshape(cores * n, rows, column...  13.4 us
    ppermute x1, waiting for transfers between devices, spread_piece(): crossed = lax.ppermute(piece, 'cand', cand_pairs(lambda x, z: (x, z ^ 2)))  11.4 us
    ppermute x2, starting transfers between devices, pair_sums(): other_got = lax.ppermute(other_sent, 'tensor', down)  10.1 us
  transfers between devices with their start and end apart: 17, of which 6 were waited for; matrix products, arithmetic and copies ran while one was open for 2% of the time, Pallas kernels for 15%

profile of v2, /device:TPU:1, one launch (start us, length us, event | category | flops | bytes accessed | tf_op | source)
XLA Modules:
  0.0 162.7 jit_solution(14157097993356352690)
XLA Ops:
  0.0 6.9 %all-to-all-start = ((bf16[8,1024,128]{2,1,0:T(8,128)(2,1)}), bf16[8,1024,128]{2,1,0:T(8,128)(2,1)}, u32[]{:S(2)}, u32[]{:S(2)}) async-start(bf16[8,1024,128]{2,1,0:T(8,128)(2,1)} %bitcast.35), calls=%async_computation | async-start | bytes 4194304 | tf_op jit(solution)/shard_map/all_to_all | solution.py:152
  6.9 6.5 %collective-permute-start = (bf16[1024,1024]{1,0:T(8,128)(2,1)S(1)}, bf16[1024,1024]{1,0:T(8,128)(2,1)}, u32[]{:S(2)}, u32[]{:S(2)}) collective-permute-start(bf16[1024,1024]{1,0:T(8,128)(2,1)S(1)} %copy-done), channel_id=1, source_target_pairs={{0,8},{8,0},{16,24},{24,16},{1,9},{9,1},{17,25},{25,17},{2,10},{10... | collective-permute-start | bytes 6291464 | tf_op jit(solution)/shard_map/ppermute | solution.py:232
  14.1 18.1 %all-to-all-done = bf16[8,1024,128]{2,1,0:T(8,128)(2,1)} async-done(((bf16[8,1024,128]{2,1,0:T(8,128)(2,1)}), bf16[8,1024,128]{2,1,0:T(8,128)(2,1)}, u32[]{:S(2)}, u32[]{:S(2)}) %all-to-all-start) | async-done | bytes 2097184 | tf_op jit(solution)/shard_map/all_to_all | solution.py:152
  33.2 6.8 %collective-permute-start.1 = (bf16[1024,128]{1,0:T(8,128)(2,1)S(1)}, bf16[1024,128]{1,0:T(8,128)(2,1)S(1)}, u32[]{:S(2)}, u32[]{:S(2)}) collective-permute-start(bf16[1024,128]{1,0:T(8,128)(2,1)S(1)} %dynamic-slice_bitcast_fusion), channel_id=1, source_target_pairs={{0,64},{32,96},{64,0},{96,32},{128,192},{160,224},{192,128},{224,1... | collective-permute-start | bytes 786440 | tf_op jit(solution)/shard_map/ppermute | solution.py:158
  40.0 11.4 %collective-permute-done.1 = bf16[1024,128]{1,0:T(8,128)(2,1)S(1)} collective-permute-done((bf16[1024,128]{1,0:T(8,128)(2,1)S(1)}, bf16[1024,128]{1,0:T(8,128)(2,1)S(1)}, u32[]{:S(2)}, u32[]{:S(2)}) %collective-permute-start.1) | collective-permute-done | bytes 262176 | tf_op jit(solution)/shard_map/ppermute | solution.py:158
  51.4 1.0 broadcast_select_fusion.refs_2_
  52.4 3.2 %collective-permute-start.4 = (bf16[1024,128]{1,0:T(8,128)(2,1)S(1)}, bf16[1024,128]{1,0:T(8,128)(2,1)S(1)}, u32[]{:S(2)}, u32[]{:S(2)}) collective-permute-start(bf16[1024,128]{1,0:T(8,128)(2,1)S(1)} %broadcast_select_fusion.refs_2_), channel_id=1, source_target_pairs={{0,32},{32,0},{64,96},{96,64},{128,160},{160,128},{192,224},{224,1... | collective-permute-start | bytes 786440 | tf_op jit(solution)/shard_map/ppermute | solution.py:245
  55.7 2.6 %collective-permute-start.2 = (bf16[1024,128]{1,0:T(8,128)(2,1)S(1)}, bf16[1024,128]{1,0:T(8,128)(2,1)S(1)}, u32[]{:S(2)}, u32[]{:S(2)}) collective-permute-start(bf16[1024,128]{1,0:T(8,128)(2,1)S(1)} %broadcast_select_fusion.refs_2_), channel_id=1, source_target_pairs={{0,384},{32,416},{64,448},{96,480},{128,0},{160,32},{192,64},{224,... | collective-permute-start | bytes 786440 | tf_op jit(solution)/shard_map/ppermute | solution.py:236
  59.0 2.7 %collective-permute-start.7 = (bf16[1024,128]{1,0:T(8,128)(2,1)S(1)}, bf16[1024,128]{1,0:T(8,128)(2,1)}, u32[]{:S(2)}, u32[]{:S(2)}) collective-permute-start(bf16[1024,128]{1,0:T(8,128)(2,1)S(1)} %broadcast_select_fusion.refs_2_), channel_id=1, source_target_pairs={{0,128},{32,160},{64,192},{96,224},{128,256},{160,288},{192,320},{... | collective-permute-start | bytes 786440 | tf_op jit(solution)/shard_map/ppermute | solution.py:236
  61.7 1.9 %collective-permute-start.5 = (bf16[1024,128]{1,0:T(8,128)(2,1)S(1)}, bf16[1024,128]{1,0:T(8,128)(2,1)}, u32[]{:S(2)}, u32[]{:S(2)}) collective-permute-start(bf16[1024,128]{1,0:T(8,128)(2,1)S(1)} %collective-permute-done.4.refs_3_), channel_id=1, source_target_pairs={{0,128},{32,160},{64,192},{96,224},{128,256},{160,288},{192,320},{... | collective-permute-start | bytes 786440 | tf_op jit(solution)/shard_map/ppermute | solution.py:236
  63.7 4.6 %collective-permute-start.8 = (bf16[1024,128]{1,0:T(8,128)(2,1)S(1)}, bf16[1024,128]{1,0:T(8,128)(2,1)}, u32[]{:S(2)}, u32[]{:S(2)}) collective-permute-start(bf16[1024,128]{1,0:T(8,128)(2,1)S(1)} %collective-permute-done.4.refs_3_), channel_id=1, source_target_pairs={{0,384},{32,416},{64,448},{96,480},{128,0},{160,32},{192,64},{224,... | collective-permute-start | bytes 786440 | tf_op jit(solution)/shard_map/ppermute | solution.py:236
  68.3 2.5 %collective-permute-start.3 = (bf16[1024,128]{1,0:T(8,128)(2,1)S(1)}, bf16[1024,128]{1,0:T(8,128)(2,1)S(1)}, u32[]{:S(2)}, u32[]{:S(2)}) collective-permute-start(bf16[1024,128]{1,0:T(8,128)(2,1)S(1)} %collective-permute-done.2.refs_4_), channel_id=1, source_target_pairs={{0,384},{32,416},{64,448},{96,480},{128,0},{160,32},{192,64},{224,... | collective-permute-start | bytes 786440 | tf_op jit(solution)/shard_map/ppermute | solution.py:236
  70.9 3.8 %shard_map.64 = (f32[256,1024]{1,0:T(8,128)S(1)}, f32[256,1024]{1,0:T(8,128)S(1)}, f32[256,1024]{1,0:T(8,128)S(1)}) custom-call(s32[2]{0:T(128)S(1)} %pad_add_fusion.1.refs_0_, bf16[256,1024]{1,0:T(8,128)(2,1)S(1)} %bitcast.31, bf16[1024,128]{1,0:T(8,128)(2,1)S(1)} %broadcast_select_fusion.refs_2_, bf16[1024,128]{1,0:T(8,128)(2,1)S(1)} %collective-permute-done.4.refs_3_, ...), custom_call_target="tpu_custom_call" | custom-call | flops 2684354560 | bytes 4194304 | tf_op jit(solution)/shard_map/pallas_call | solution.py:130
  74.7 2.9 %collective-permute-start.6 = (bf16[1024,128]{1,0:T(8,128)(2,1)}, bf16[1024,128]{1,0:T(8,128)(2,1)S(1)}, u32[]{:S(2)}, u32[]{:S(2)}) collective-permute-start(bf16[1024,128]{1,0:T(8,128)(2,1)} %collective-permute-done.5.refs_3_), channel_id=1, source_target_pairs={{0,128},{32,160},{64,192},{96,224},{128,256},{160,288},{192,320},{... | collective-permute-start | bytes 786440 | tf_op jit(solution)/shard_map/ppermute | solution.py:236
  77.7 6.3 %shard_map.65 = (f32[256,1024]{1,0:T(8,128)S(1)}, f32[256,1024]{1,0:T(8,128)S(1)}, f32[256,1024]{1,0:T(8,128)S(1)}) custom-call(s32[2]{0:T(128)S(1)} %pad_add_fusion.1.refs_0_, bf16[256,1024]{1,0:T(8,128)(2,1)S(1)} %bitcast.32, bf16[1024,128]{1,0:T(8,128)(2,1)} %collective-permute-done.7.refs_2_, bf16[1024,128]{1,0:T(8,128)(2,1)} %collective-permute-done.5.refs_3_, ...), custom_call_target="tpu_custom_call" | custom-call | flops 4294967296 | bytes 4194304 | tf_op jit(solution)/shard_map/pallas_call | solution.py:130
  84.0 3.5 %shard_map.66.refs_3_ = bf16[256,1024]{1,0:T(8,128)(2,1)S(1)} custom-call(s32[2]{0:T(128)S(1)} %pad_add_fusion.1.refs_0_, bf16[256,1024]{1,0:T(8,128)(2,1)S(1)} %bitcast.33, bf16[1024,128]{1,0:T(8,128)(2,1)S(1)} %collective-permute-done.3.refs_2_, bf16[1024,128]{1,0:T(8,128)(2,1)S(1)} %collective-permute-done.6.refs_3_, ...), custom_call_target="tpu_custom_call" | custom-call | flops 2147483648 | bytes 4194304 | tf_op jit(solution)/shard_map/pallas_call | solution.py:130
  87.5 7.9 %collective-permute-start.11 = (bf16[256,1024]{1,0:T(8,128)(2,1)S(1)}, bf16[256,1024]{1,0:T(8,128)(2,1)S(1)}, u32[]{:S(2)}, u32[]{:S(2)}) collective-permute-start(bf16[256,1024]{1,0:T(8,128)(2,1)S(1)} %shard_map.66.refs_3_), channel_id=1, source_target_pairs={{0,16},{8,24},{16,0},{24,8},{1,17},{9,25},{17,1},{25,9},{2,18},{10... | collective-permute-start | bytes 1572872 | tf_op jit(solution)/shard_map/ppermute | solution.py:232
  95.5 2.5 %shard_map.68 = (bf16[4,256,128]{2,1,0:T(8,128)(2,1)S(1)}, bf16[4,256,128]{2,1,0:T(8,128)(2,1)S(1)}) custom-call(s32[2]{0:T(128)S(1)} %pad_add_fusion.refs_0_, bf16[1024,1024]{1,0:T(8,128)(2,1)S(1)} %copy-done, bf16[1024,1024]{1,0:T(8,128)(2,1)} %collective-permute-done.refs_2_, bf16[256,1024]{1,0:T(8,128)(2,1)S(1)} %shard_map.66.refs_3_), custom_call_target="tpu_custom_call" | custom-call | flops 21474836480 | bytes 4194304 | tf_op jit(solution)/shard_map/pallas_call | solution.py:186
  98.0 5.1 %collective-permute-start.10 = (bf16[4,256,128]{2,1,0:T(8,128)(2,1)S(1)}, bf16[4,256,128]{2,1,0:T(8,128)(2,1)S(1)}, u32[]{:S(2)}, u32[]{:S(2)}) collective-permute-start(bf16[4,256,128]{2,1,0:T(8,128)(2,1)S(1)} %get-tuple-element.24), channel_id=1, source_target_pairs={{0,7},{1,2},{2,1},{3,4},{4,3},{5,6},{6,5},{7,0},{8,15},{9,10},{10,... | collective-permute-start | bytes 786440 | tf_op jit(solution)/shard_map/ppermute | solution.py:206
  103.1 1.9 %collective-permute-start.9 = (bf16[4,256,128]{2,1,0:T(8,128)(2,1)S(1)}, bf16[4,256,128]{2,1,0:T(8,128)(2,1)S(1)}, u32[]{:S(2)}, u32[]{:S(2)}) collective-permute-start(bf16[4,256,128]{2,1,0:T(8,128)(2,1)S(1)} %get-tuple-element.23), channel_id=1, source_target_pairs={{0,1},{1,0},{2,3},{3,2},{4,5},{5,4},{6,7},{7,6},{8,9},{9,8},{10,11... | collective-permute-start | bytes 786440 | tf_op jit(solution)/shard_map/ppermute | solution.py:205
  105.0 2.5 %shard_map.67 = f32[2,4,256,128]{3,2,1,0:T(8,128)S(1)} custom-call(s32[2]{0:T(128)S(1)} %pad_add_fusion.refs_0_, bf16[1024,1024]{1,0:T(8,128)(2,1)S(1)} %copy-done, bf16[1024,1024]{1,0:T(8,128)(2,1)} %collective-permute-done.refs_2_, bf16[256,1024]{1,0:T(8,128)(2,1)S(1)} %shard_map.66.refs_3_), custom_call_target="tpu_custom_call" | custom-call | flops 21474836480 | bytes 4194304 | tf_op jit(solution)/shard_map/pallas_call | solution.py:186
  107.5 2.8 %collective-permute-done.9 = bf16[4,256,128]{2,1,0:T(8,128)(2,1)S(1)} collective-permute-done((bf16[4,256,128]{2,1,0:T(8,128)(2,1)S(1)}, bf16[4,256,128]{2,1,0:T(8,128)(2,1)S(1)}, u32[]{:S(2)}, u32[]{:S(2)}) %collective-permute-start.9) | collective-permute-done | bytes 262176 | tf_op jit(solution)/shard_map/ppermute | solution.py:205
  111.2 8.4 %all-to-all-start.1 = ((bf16[8,256,128]{2,1,0:T(8,128)(2,1)}), bf16[8,256,128]{2,1,0:T(8,128)(2,1)}, u32[]{:S(2)}, u32[]{:S(2)}) async-start(bf16[8,256,128]{2,1,0:T(8,128)(2,1)} %bitcast.36), calls=%async_computation.1 | async-start | bytes 1048576 | tf_op jit(solution)/shard_map/all_to_all | solution.py:220
  119.7 2.5 %shard_map.70 = (bf16[4,256,128]{2,1,0:T(8,128)(2,1)S(1)}, bf16[4,256,128]{2,1,0:T(8,128)(2,1)S(1)}) custom-call(s32[2]{0:T(128)S(1)} %pad_add_fusion.refs_0_, bf16[1024,1024]{1,0:T(8,128)(2,1)S(1)} %copy-done, bf16[1024,1024]{1,0:T(8,128)(2,1)} %collective-permute-done.refs_2_, bf16[256,1024]{1,0:T(8,128)(2,1)S(1)} %collective-permute-done.11.refs_3_), custom_call_target="tpu_custom_call" | custom-call | flops 21474836480 | bytes 4194304 | tf_op jit(solution)/shard_map/pallas_call | solution.py:186
  122.2 2.5 %collective-permute-start.12 = (bf16[4,256,128]{2,1,0:T(8,128)(2,1)S(1)}, bf16[4,256,128]{2,1,0:T(8,128)(2,1)S(1)}, u32[]{:S(2)}, u32[]{:S(2)}) collective-permute-start(bf16[4,256,128]{2,1,0:T(8,128)(2,1)S(1)} %get-tuple-element.26), channel_id=1, source_target_pairs={{0,1},{1,0},{2,3},{3,2},{4,5},{5,4},{6,7},{7,6},{8,9},{9,8},{10,11... | collective-permute-start | bytes 786440 | tf_op jit(solution)/shard_map/ppermute | solution.py:205
  124.7 5.1 %collective-permute-start.13 = (bf16[4,256,128]{2,1,0:T(8,128)(2,1)S(1)}, bf16[4,256,128]{2,1,0:T(8,128)(2,1)S(1)}, u32[]{:S(2)}, u32[]{:S(2)}) collective-permute-start(bf16[4,256,128]{2,1,0:T(8,128)(2,1)S(1)} %get-tuple-element.27), channel_id=1, source_target_pairs={{0,7},{1,2},{2,1},{3,4},{4,3},{5,6},{6,5},{7,0},{8,15},{9,10},{10,... | collective-permute-start | bytes 786440 | tf_op jit(solution)/shard_map/ppermute | solution.py:206
  129.8 2.5 %shard_map.69 = f32[2,4,256,128]{3,2,1,0:T(8,128)S(1)} custom-call(s32[2]{0:T(128)S(1)} %pad_add_fusion.refs_0_, bf16[1024,1024]{1,0:T(8,128)(2,1)S(1)} %copy-done, bf16[1024,1024]{1,0:T(8,128)(2,1)} %collective-permute-done.refs_2_, bf16[256,1024]{1,0:T(8,128)(2,1)S(1)} %collective-permute-done.11.refs_3_), custom_call_target="tpu_custom_call" | custom-call | flops 21474836480 | bytes 4194304 | tf_op jit(solution)/shard_map/pallas_call | solution.py:186
  132.3 6.1 %collective-permute-done.12 = bf16[4,256,128]{2,1,0:T(8,128)(2,1)S(1)} collective-permute-done((bf16[4,256,128]{2,1,0:T(8,128)(2,1)S(1)}, bf16[4,256,128]{2,1,0:T(8,128)(2,1)S(1)}, u32[]{:S(2)}, u32[]{:S(2)}) %collective-permute-start.12) | collective-permute-done | bytes 262176 | tf_op jit(solution)/shard_map/ppermute | solution.py:205
  138.4 2.0 %collective-permute-done.13 = bf16[4,256,128]{2,1,0:T(8,128)(2,1)S(1)} collective-permute-done((bf16[4,256,128]{2,1,0:T(8,128)(2,1)S(1)}, bf16[4,256,128]{2,1,0:T(8,128)(2,1)S(1)}, u32[]{:S(2)}, u32[]{:S(2)}) %collective-permute-start.13) | collective-permute-done | bytes 262176 | tf_op jit(solution)/shard_map/ppermute | solution.py:206
  141.4 1.1 bitcast_reduce_fusion.1
  142.5 5.0 %all-to-all-start.2 = ((bf16[8,256,128]{2,1,0:T(8,128)(2,1)}), bf16[8,256,128]{2,1,0:T(8,128)(2,1)S(1)}, u32[]{:S(2)}, u32[]{:S(2)}) async-start(bf16[8,256,128]{2,1,0:T(8,128)(2,1)} %bitcast.15), calls=%async_computation.2 | async-start | bytes 1048576 | tf_op jit(solution)/shard_map/all_to_all | solution.py:220
  147.6 14.3 %all-to-all-done.2 = bf16[8,256,128]{2,1,0:T(8,128)(2,1)S(1)} async-done(((bf16[8,256,128]{2,1,0:T(8,128)(2,1)}), bf16[8,256,128]{2,1,0:T(8,128)(2,1)S(1)}, u32[]{:S(2)}, u32[]{:S(2)}) %all-to-all-start.2) | async-done | bytes 524320 | tf_op jit(solution)/shard_map/all_to_all | solution.py:220
  (27 shorter events, 3.9 us)
Async XLA Ops:
  0.0 6.9 %copy-start = (bf16[1024,1024]{1,0:T(8,128)(2,1)S(1)}, bf16[1024,1024]{1,0:T(8,128)(2,1)}, u32[]{:S(2)}) copy-start(bf16[1024,1024]{1,0:T(8,128)(2,1)} %refs_1_.7) | copy-start | bytes 6291460
  0.0 70.9 %copy-start.1 = (bf16[1,256,1024]{2,1,0:T(8,128)(2,1)S(1)}, bf16[1,256,1024]{2,1,0:T(8,128)(2,1)}, u32[]{:S(2)}) copy-start(bf16[1,256,1024]{2,1,0:T(8,128)(2,1)} %param.8) | copy-start | bytes 1572868
  0.0 70.9 %copy-start.2 = (bf16[2,1,256,128]{3,2,1,0:T(8,128)(2,1)S(1)}, bf16[2,1,256,128]{3,2,1,0:T(8,128)(2,1)}, u32[]{:S(2)}) copy-start(bf16[2,1,256,128]{3,2,1,0:T(8,128)(2,1)} %param.9) | copy-start | bytes 393220
  0.0 32.2 %all-to-all-start = ((bf16[8,1024,128]{2,1,0:T(8,128)(2,1)}), bf16[8,1024,128]{2,1,0:T(8,128)(2,1)}, u32[]{:S(2)}, u32[]{:S(2)}) async-start(bf16[8,1024,128]{2,1,0:T(8,128)(2,1)} %bitcast.35), calls=%async_computation | async-start | bytes 4194304 | tf_op jit(solution)/shard_map/all_to_all | solution.py:152
  6.9 88.5 %collective-permute-start = (bf16[1024,1024]{1,0:T(8,128)(2,1)S(1)}, bf16[1024,1024]{1,0:T(8,128)(2,1)}, u32[]{:S(2)}, u32[]{:S(2)}) collective-permute-start(bf16[1024,1024]{1,0:T(8,128)(2,1)S(1)} %copy-done), channel_id=1, source_target_pairs={{0,8},{8,0},{16,24},{24,16},{1,9},{9,1},{17,25},{25,17},{2,10},{10... | collective-permute-start | bytes 6291464 | tf_op jit(solution)/shard_map/ppermute | solution.py:232
  33.2 18.3 %collective-permute-start.1 = (bf16[1024,128]{1,0:T(8,128)(2,1)S(1)}, bf16[1024,128]{1,0:T(8,128)(2,1)S(1)}, u32[]{:S(2)}, u32[]{:S(2)}) collective-permute-start(bf16[1024,128]{1,0:T(8,128)(2,1)S(1)} %dynamic-slice_bitcast_fusion), channel_id=1, source_target_pairs={{0,64},{32,96},{64,0},{96,32},{128,192},{160,224},{192,128},{224,1... | collective-permute-start | bytes 786440 | tf_op jit(solution)/shard_map/ppermute | solution.py:158
  52.4 9.3 %collective-permute-start.4 = (bf16[1024,128]{1,0:T(8,128)(2,1)S(1)}, bf16[1024,128]{1,0:T(8,128)(2,1)S(1)}, u32[]{:S(2)}, u32[]{:S(2)}) collective-permute-start(bf16[1024,128]{1,0:T(8,128)(2,1)S(1)} %broadcast_select_fusion.refs_2_), channel_id=1, source_target_pairs={{0,32},{32,0},{64,96},{96,64},{128,160},{160,128},{192,224},{224,1... | collective-permute-start | bytes 786440 | tf_op jit(solution)/shard_map/ppermute | solution.py:245
  55.7 12.6 %collective-permute-start.2 = (bf16[1024,128]{1,0:T(8,128)(2,1)S(1)}, bf16[1024,128]{1,0:T(8,128)(2,1)S(1)}, u32[]{:S(2)}, u32[]{:S(2)}) collective-permute-start(bf16[1024,128]{1,0:T(8,128)(2,1)S(1)} %broadcast_select_fusion.refs_2_), channel_id=1, source_target_pairs={{0,384},{32,416},{64,448},{96,480},{128,0},{160,32},{192,64},{224,... | collective-permute-start | bytes 786440 | tf_op jit(solution)/shard_map/ppermute | solution.py:236
  59.0 18.6 %collective-permute-start.7 = (bf16[1024,128]{1,0:T(8,128)(2,1)S(1)}, bf16[1024,128]{1,0:T(8,128)(2,1)}, u32[]{:S(2)}, u32[]{:S(2)}) collective-permute-start(bf16[1024,128]{1,0:T(8,128)(2,1)S(1)} %broadcast_select_fusion.refs_2_), channel_id=1, source_target_pairs={{0,128},{32,160},{64,192},{96,224},{128,256},{160,288},{192,320},{... | collective-permute-start | bytes 786440 | tf_op jit(solution)/shard_map/ppermute | solution.py:236
  61.7 13.0 %collective-permute-start.5 = (bf16[1024,128]{1,0:T(8,128)(2,1)S(1)}, bf16[1024,128]{1,0:T(8,128)(2,1)}, u32[]{:S(2)}, u32[]{:S(2)}) collective-permute-start(bf16[1024,128]{1,0:T(8,128)(2,1)S(1)} %collective-permute-done.4.refs_3_), channel_id=1, source_target_pairs={{0,128},{32,160},{64,192},{96,224},{128,256},{160,288},{192,320},{... | collective-permute-start | bytes 786440 | tf_op jit(solution)/shard_map/ppermute | solution.py:236
  63.7 14.0 %collective-permute-start.8 = (bf16[1024,128]{1,0:T(8,128)(2,1)S(1)}, bf16[1024,128]{1,0:T(8,128)(2,1)}, u32[]{:S(2)}, u32[]{:S(2)}) collective-permute-start(bf16[1024,128]{1,0:T(8,128)(2,1)S(1)} %collective-permute-done.4.refs_3_), channel_id=1, source_target_pairs={{0,384},{32,416},{64,448},{96,480},{128,0},{160,32},{192,64},{224,... | collective-permute-start | bytes 786440 | tf_op jit(solution)/shard_map/ppermute | solution.py:236
  68.3 15.7 %collective-permute-start.3 = (bf16[1024,128]{1,0:T(8,128)(2,1)S(1)}, bf16[1024,128]{1,0:T(8,128)(2,1)S(1)}, u32[]{:S(2)}, u32[]{:S(2)}) collective-permute-start(bf16[1024,128]{1,0:T(8,128)(2,1)S(1)} %collective-permute-done.2.refs_4_), channel_id=1, source_target_pairs={{0,384},{32,416},{64,448},{96,480},{128,0},{160,32},{192,64},{224,... | collective-permute-start | bytes 786440 | tf_op jit(solution)/shard_map/ppermute | solution.py:236
  74.7 9.3 %collective-permute-start.6 = (bf16[1024,128]{1,0:T(8,128)(2,1)}, bf16[1024,128]{1,0:T(8,128)(2,1)S(1)}, u32[]{:S(2)}, u32[]{:S(2)}) collective-permute-start(bf16[1024,128]{1,0:T(8,128)(2,1)} %collective-permute-done.5.refs_3_), channel_id=1, source_target_pairs={{0,128},{32,160},{64,192},{96,224},{128,256},{160,288},{192,320},{... | collective-permute-start | bytes 786440 | tf_op jit(solution)/shard_map/ppermute | solution.py:236
  87.5 32.2 %collective-permute-start.11 = (bf16[256,1024]{1,0:T(8,128)(2,1)S(1)}, bf16[256,1024]{1,0:T(8,128)(2,1)S(1)}, u32[]{:S(2)}, u32[]{:S(2)}) collective-permute-start(bf16[256,1024]{1,0:T(8,128)(2,1)S(1)} %shard_map.66.refs_3_), channel_id=1, source_target_pairs={{0,16},{8,24},{16,0},{24,8},{1,17},{9,25},{17,1},{25,9},{2,18},{10... | collective-permute-start | bytes 1572872 | tf_op jit(solution)/shard_map/ppermute | solution.py:232
  98.0 9.6 %collective-permute-start.10 = (bf16[4,256,128]{2,1,0:T(8,128)(2,1)S(1)}, bf16[4,256,128]{2,1,0:T(8,128)(2,1)S(1)}, u32[]{:S(2)}, u32[]{:S(2)}) collective-permute-start(bf16[4,256,128]{2,1,0:T(8,128)(2,1)S(1)} %get-tuple-element.24), channel_id=1, source_target_pairs={{0,7},{1,2},{2,1},{3,4},{4,3},{5,6},{6,5},{7,0},{8,15},{9,10},{10,... | collective-permute-start | bytes 786440 | tf_op jit(solution)/shard_map/ppermute | solution.py:206
  103.1 7.2 %collective-permute-start.9 = (bf16[4,256,128]{2,1,0:T(8,128)(2,1)S(1)}, bf16[4,256,128]{2,1,0:T(8,128)(2,1)S(1)}, u32[]{:S(2)}, u32[]{:S(2)}) collective-permute-start(bf16[4,256,128]{2,1,0:T(8,128)(2,1)S(1)} %get-tuple-element.23), channel_id=1, source_target_pairs={{0,1},{1,0},{2,3},{3,2},{4,5},{5,4},{6,7},{7,6},{8,9},{9,8},{10,11... | collective-permute-start | bytes 786440 | tf_op jit(solution)/shard_map/ppermute | solution.py:205
  111.2 30.2 %all-to-all-start.1 = ((bf16[8,256,128]{2,1,0:T(8,128)(2,1)}), bf16[8,256,128]{2,1,0:T(8,128)(2,1)}, u32[]{:S(2)}, u32[]{:S(2)}) async-start(bf16[8,256,128]{2,1,0:T(8,128)(2,1)} %bitcast.36), calls=%async_computation.1 | async-start | bytes 1048576 | tf_op jit(solution)/shard_map/all_to_all | solution.py:220
  122.2 16.3 %collective-permute-start.12 = (bf16[4,256,128]{2,1,0:T(8,128)(2,1)S(1)}, bf16[4,256,128]{2,1,0:T(8,128)(2,1)S(1)}, u32[]{:S(2)}, u32[]{:S(2)}) collective-permute-start(bf16[4,256,128]{2,1,0:T(8,128)(2,1)S(1)} %get-tuple-element.26), channel_id=1, source_target_pairs={{0,1},{1,0},{2,3},{3,2},{4,5},{5,4},{6,7},{7,6},{8,9},{9,8},{10,11... | collective-permute-start | bytes 786440 | tf_op jit(solution)/shard_map/ppermute | solution.py:205
  124.7 15.8 %collective-permute-start.13 = (bf16[4,256,128]{2,1,0:T(8,128)(2,1)S(1)}, bf16[4,256,128]{2,1,0:T(8,128)(2,1)S(1)}, u32[]{:S(2)}, u32[]{:S(2)}) collective-permute-start(bf16[4,256,128]{2,1,0:T(8,128)(2,1)S(1)} %get-tuple-element.27), channel_id=1, source_target_pairs={{0,7},{1,2},{2,1},{3,4},{4,3},{5,6},{6,5},{7,0},{8,15},{9,10},{10,... | collective-permute-start | bytes 786440 | tf_op jit(solution)/shard_map/ppermute | solution.py:206
  142.5 19.4 %all-to-all-start.2 = ((bf16[8,256,128]{2,1,0:T(8,128)(2,1)}), bf16[8,256,128]{2,1,0:T(8,128)(2,1)S(1)}, u32[]{:S(2)}, u32[]{:S(2)}) async-start(bf16[8,256,128]{2,1,0:T(8,128)(2,1)} %bitcast.15), calls=%async_computation.2 | async-start | bytes 1048576 | tf_op jit(solution)/shard_map/all_to_all | solution.py:220

commit v3 on v2

--- a/solution.py
+++ b/solution.py
@@ -224,8 +224,11 @@
         concat_axis=0,
         axis_index_groups=groups,
     )
-    terms = terms.reshape(cores, n, rows, columns).astype(jnp.float32)
-    return terms.sum(axis=1).astype(jnp.bfloat16)
+    return terms.reshape(cores, n, rows, columns)
+
+
+def add_up(terms):
+    return terms.astype(jnp.float32).sum(axis=1).astype(jnp.bfloat16)
 
 
 def swap(value, bit):
@@ -254,8 +257,9 @@
     near_terms = pair_sums(attended, *weights)
     near = exchange(near_terms)
     _, far_rows = lax.optimization_barrier((near_terms, far_rows))
-    far_terms, _ = lax.optimization_barrier((pair_sums(far_rows, *weights), near))
-    far = exchange(far_terms)
+    far_terms, near = lax.optimization_barrier((pair_sums(far_rows, *weights), near))
+    far = add_up(exchange(far_terms))
+    near = add_up(near)
     first = lax.axis_index("prompt") < 2
     return jnp.concatenate([jnp.where(first, near, far), jnp.where(first, far, near)])
 

time: 165 us -> 164 us (level)
  transfers between devices with their start and end apart: 17 -> 17, of which waited for: 6 -> 6; matrix products, arithmetic and copies ran while one was open for 2% -> 3% of each run, Pallas kernels for 15% -> 15%
where the time goes in v3:
time: 164 us; the launch traced here: 162 us
  starting transfers between devices  76.7 us (47%)
  waiting for transfers between devices  53.6 us (33%)
  Pallas kernels  23.7 us (14%)
  other arithmetic  4.97 us (3%)
  between operations  1.72 us (1%)
    all_to_all x1, waiting for transfers between devices, spread_piece(): lax.all_to_all(pieces, 'cand', split_axis=0, concat_axis=0, axis_index_gr...  18.1 us
    ppermute x6, starting transfers between devices, move(): return lax.ppermute(value, 'cand', cand_pairs(lambda x, z: (x + shift, z)))  17.2 us
    ppermute x2, starting transfers between devices, swap(): return lax.ppermute(value, 'prompt', [(p, p ^ bit) for p in range(4)])  14.4 us
    pallas_call x3, Pallas kernels, attend(): pl.pallas_call(lambda *refs: attention_kernel(len(blocks), suffix is not...  13.6 us
    all_to_all x2, starting transfers between devices, exchange(): lax.all_to_all(terms.astype(jnp.bfloat16).reshape(cores * n, rows, column...  13.4 us
    all_to_all x2, waiting for transfers between devices, exchange(): lax.all_to_all(terms.astype(jnp.bfloat16).reshape(cores * n, rows, column...  13.2 us
    ppermute x1, waiting for transfers between devices, spread_piece(): crossed = lax.ppermute(piece, 'cand', cand_pairs(lambda x, z: (x, z ^ 2)))  11.4 us
    ppermute x2, starting transfers between devices, pair_sums(): other_got = lax.ppermute(other_sent, 'tensor', down)  10.1 us
  transfers between devices with their start and end apart: 17, of which 6 were waited for; matrix products, arithmetic and copies ran while one was open for 3% of the time, Pallas kernels for 15%

profile of v3, /device:TPU:1, one launch (start us, length us, event | category | flops | bytes accessed | tf_op | source)
XLA Modules:
  0.0 161.6 jit_solution(6196948106333842246)
XLA Ops:
  0.0 6.9 %all-to-all-start = ((bf16[8,1024,128]{2,1,0:T(8,128)(2,1)}), bf16[8,1024,128]{2,1,0:T(8,128)(2,1)}, u32[]{:S(2)}, u32[]{:S(2)}) async-start(bf16[8,1024,128]{2,1,0:T(8,128)(2,1)} %bitcast.34), calls=%async_computation | async-start | bytes 4194304 | tf_op jit(solution)/shard_map/all_to_all | solution.py:152
  6.9 6.5 %collective-permute-start = (bf16[1024,1024]{1,0:T(8,128)(2,1)S(1)}, bf16[1024,1024]{1,0:T(8,128)(2,1)}, u32[]{:S(2)}, u32[]{:S(2)}) collective-permute-start(bf16[1024,1024]{1,0:T(8,128)(2,1)S(1)} %copy-done), channel_id=1, source_target_pairs={{0,8},{8,0},{16,24},{24,16},{1,9},{9,1},{17,25},{25,17},{2,10},{10... | collective-permute-start | bytes 6291464 | tf_op jit(solution)/shard_map/ppermute | solution.py:235
  14.1 18.1 %all-to-all-done = bf16[8,1024,128]{2,1,0:T(8,128)(2,1)} async-done(((bf16[8,1024,128]{2,1,0:T(8,128)(2,1)}), bf16[8,1024,128]{2,1,0:T(8,128)(2,1)}, u32[]{:S(2)}, u32[]{:S(2)}) %all-to-all-start) | async-done | bytes 2097184 | tf_op jit(solution)/shard_map/all_to_all | solution.py:152
  33.2 6.8 %collective-permute-start.1 = (bf16[1024,128]{1,0:T(8,128)(2,1)S(1)}, bf16[1024,128]{1,0:T(8,128)(2,1)S(1)}, u32[]{:S(2)}, u32[]{:S(2)}) collective-permute-start(bf16[1024,128]{1,0:T(8,128)(2,1)S(1)} %dynamic-slice_bitcast_fusion), channel_id=1, source_target_pairs={{0,64},{32,96},{64,0},{96,32},{128,192},{160,224},{192,128},{224,1... | collective-permute-start | bytes 786440 | tf_op jit(solution)/shard_map/ppermute | solution.py:158
  40.0 11.4 %collective-permute-done.1 = bf16[1024,128]{1,0:T(8,128)(2,1)S(1)} collective-permute-done((bf16[1024,128]{1,0:T(8,128)(2,1)S(1)}, bf16[1024,128]{1,0:T(8,128)(2,1)S(1)}, u32[]{:S(2)}, u32[]{:S(2)}) %collective-permute-start.1) | collective-permute-done | bytes 262176 | tf_op jit(solution)/shard_map/ppermute | solution.py:158
  51.4 1.0 broadcast_select_fusion.refs_2_
  52.4 3.2 %collective-permute-start.4 = (bf16[1024,128]{1,0:T(8,128)(2,1)S(1)}, bf16[1024,128]{1,0:T(8,128)(2,1)S(1)}, u32[]{:S(2)}, u32[]{:S(2)}) collective-permute-start(bf16[1024,128]{1,0:T(8,128)(2,1)S(1)} %broadcast_select_fusion.refs_2_), channel_id=1, source_target_pairs={{0,32},{32,0},{64,96},{96,64},{128,160},{160,128},{192,224},{224,1... | collective-permute-start | bytes 786440 | tf_op jit(solution)/shard_map/ppermute | solution.py:248
  55.7 2.6 %collective-permute-start.2 = (bf16[1024,128]{1,0:T(8,128)(2,1)S(1)}, bf16[1024,128]{1,0:T(8,128)(2,1)S(1)}, u32[]{:S(2)}, u32[]{:S(2)}) collective-permute-start(bf16[1024,128]{1,0:T(8,128)(2,1)S(1)} %broadcast_select_fusion.refs_2_), channel_id=1, source_target_pairs={{0,384},{32,416},{64,448},{96,480},{128,0},{160,32},{192,64},{224,... | collective-permute-start | bytes 786440 | tf_op jit(solution)/shard_map/ppermute | solution.py:239
  59.0 2.7 %collective-permute-start.7 = (bf16[1024,128]{1,0:T(8,128)(2,1)S(1)}, bf16[1024,128]{1,0:T(8,128)(2,1)}, u32[]{:S(2)}, u32[]{:S(2)}) collective-permute-start(bf16[1024,128]{1,0:T(8,128)(2,1)S(1)} %broadcast_select_fusion.refs_2_), channel_id=1, source_target_pairs={{0,128},{32,160},{64,192},{96,224},{128,256},{160,288},{192,320},{... | collective-permute-start | bytes 786440 | tf_op jit(solution)/shard_map/ppermute | solution.py:239
  61.7 1.9 %collective-permute-start.5 = (bf16[1024,128]{1,0:T(8,128)(2,1)S(1)}, bf16[1024,128]{1,0:T(8,128)(2,1)}, u32[]{:S(2)}, u32[]{:S(2)}) collective-permute-start(bf16[1024,128]{1,0:T(8,128)(2,1)S(1)} %collective-permute-done.4.refs_3_), channel_id=1, source_target_pairs={{0,128},{32,160},{64,192},{96,224},{128,256},{160,288},{192,320},{... | collective-permute-start | bytes 786440 | tf_op jit(solution)/shard_map/ppermute | solution.py:239
  63.7 4.6 %collective-permute-start.8 = (bf16[1024,128]{1,0:T(8,128)(2,1)S(1)}, bf16[1024,128]{1,0:T(8,128)(2,1)}, u32[]{:S(2)}, u32[]{:S(2)}) collective-permute-start(bf16[1024,128]{1,0:T(8,128)(2,1)S(1)} %collective-permute-done.4.refs_3_), channel_id=1, source_target_pairs={{0,384},{32,416},{64,448},{96,480},{128,0},{160,32},{192,64},{224,... | collective-permute-start | bytes 786440 | tf_op jit(solution)/shard_map/ppermute | solution.py:239
  68.3 2.5 %collective-permute-start.3 = (bf16[1024,128]{1,0:T(8,128)(2,1)S(1)}, bf16[1024,128]{1,0:T(8,128)(2,1)S(1)}, u32[]{:S(2)}, u32[]{:S(2)}) collective-permute-start(bf16[1024,128]{1,0:T(8,128)(2,1)S(1)} %collective-permute-done.2.refs_4_), channel_id=1, source_target_pairs={{0,384},{32,416},{64,448},{96,480},{128,0},{160,32},{192,64},{224,... | collective-permute-start | bytes 786440 | tf_op jit(solution)/shard_map/ppermute | solution.py:239
  70.9 3.8 %shard_map.64 = (f32[256,1024]{1,0:T(8,128)S(1)}, f32[256,1024]{1,0:T(8,128)S(1)}, f32[256,1024]{1,0:T(8,128)S(1)}) custom-call(s32[2]{0:T(128)S(1)} %pad_add_fusion.1.refs_0_, bf16[256,1024]{1,0:T(8,128)(2,1)S(1)} %bitcast.30, bf16[1024,128]{1,0:T(8,128)(2,1)S(1)} %broadcast_select_fusion.refs_2_, bf16[1024,128]{1,0:T(8,128)(2,1)S(1)} %collective-permute-done.4.refs_3_, ...), custom_call_target="tpu_custom_call" | custom-call | flops 2684354560 | bytes 4194304 | tf_op jit(solution)/shard_map/pallas_call | solution.py:130
  74.7 2.9 %collective-permute-start.6 = (bf16[1024,128]{1,0:T(8,128)(2,1)}, bf16[1024,128]{1,0:T(8,128)(2,1)S(1)}, u32[]{:S(2)}, u32[]{:S(2)}) collective-permute-start(bf16[1024,128]{1,0:T(8,128)(2,1)} %collective-permute-done.5.refs_3_), channel_id=1, source_target_pairs={{0,128},{32,160},{64,192},{96,224},{128,256},{160,288},{192,320},{... | collective-permute-start | bytes 786440 | tf_op jit(solution)/shard_map/ppermute | solution.py:239
  77.7 6.3 %shard_map.65 = (f32[256,1024]{1,0:T(8,128)S(1)}, f32[256,1024]{1,0:T(8,128)S(1)}, f32[256,1024]{1,0:T(8,128)S(1)}) custom-call(s32[2]{0:T(128)S(1)} %pad_add_fusion.1.refs_0_, bf16[256,1024]{1,0:T(8,128)(2,1)S(1)} %bitcast.31, bf16[1024,128]{1,0:T(8,128)(2,1)} %collective-permute-done.7.refs_2_, bf16[1024,128]{1,0:T(8,128)(2,1)} %collective-permute-done.5.refs_3_, ...), custom_call_target="tpu_custom_call" | custom-call | flops 4294967296 | bytes 4194304 | tf_op jit(solution)/shard_map/pallas_call | solution.py:130
  84.0 3.5 %shard_map.66.refs_3_ = bf16[256,1024]{1,0:T(8,128)(2,1)S(1)} custom-call(s32[2]{0:T(128)S(1)} %pad_add_fusion.1.refs_0_, bf16[256,1024]{1,0:T(8,128)(2,1)S(1)} %bitcast.32, bf16[1024,128]{1,0:T(8,128)(2,1)S(1)} %collective-permute-done.3.refs_2_, bf16[1024,128]{1,0:T(8,128)(2,1)S(1)} %collective-permute-done.6.refs_3_, ...), custom_call_target="tpu_custom_call" | custom-call | flops 2147483648 | bytes 4194304 | tf_op jit(solution)/shard_map/pallas_call | solution.py:130
  87.5 7.9 %collective-permute-start.11 = (bf16[256,1024]{1,0:T(8,128)(2,1)S(1)}, bf16[256,1024]{1,0:T(8,128)(2,1)S(1)}, u32[]{:S(2)}, u32[]{:S(2)}) collective-permute-start(bf16[256,1024]{1,0:T(8,128)(2,1)S(1)} %shard_map.66.refs_3_), channel_id=1, source_target_pairs={{0,16},{8,24},{16,0},{24,8},{1,17},{9,25},{17,1},{25,9},{2,18},{10... | collective-permute-start | bytes 1572872 | tf_op jit(solution)/shard_map/ppermute | solution.py:235
  95.5 2.5 %shard_map.68 = (bf16[4,256,128]{2,1,0:T(8,128)(2,1)S(1)}, bf16[4,256,128]{2,1,0:T(8,128)(2,1)S(1)}) custom-call(s32[2]{0:T(128)S(1)} %pad_add_fusion.refs_0_, bf16[1024,1024]{1,0:T(8,128)(2,1)S(1)} %copy-done, bf16[1024,1024]{1,0:T(8,128)(2,1)} %collective-permute-done.refs_2_, bf16[256,1024]{1,0:T(8,128)(2,1)S(1)} %shard_map.66.refs_3_), custom_call_target="tpu_custom_call" | custom-call | flops 21474836480 | bytes 4194304 | tf_op jit(solution)/shard_map/pallas_call | solution.py:186
  98.0 5.1 %collective-permute-start.10 = (bf16[4,256,128]{2,1,0:T(8,128)(2,1)S(1)}, bf16[4,256,128]{2,1,0:T(8,128)(2,1)S(1)}, u32[]{:S(2)}, u32[]{:S(2)}) collective-permute-start(bf16[4,256,128]{2,1,0:T(8,128)(2,1)S(1)} %get-tuple-element.25), channel_id=1, source_target_pairs={{0,7},{1,2},{2,1},{3,4},{4,3},{5,6},{6,5},{7,0},{8,15},{9,10},{10,... | collective-permute-start | bytes 786440 | tf_op jit(solution)/shard_map/ppermute | solution.py:206
  103.1 1.9 %collective-permute-start.9 = (bf16[4,256,128]{2,1,0:T(8,128)(2,1)S(1)}, bf16[4,256,128]{2,1,0:T(8,128)(2,1)S(1)}, u32[]{:S(2)}, u32[]{:S(2)}) collective-permute-start(bf16[4,256,128]{2,1,0:T(8,128)(2,1)S(1)} %get-tuple-element.24), channel_id=1, source_target_pairs={{0,1},{1,0},{2,3},{3,2},{4,5},{5,4},{6,7},{7,6},{8,9},{9,8},{10,11... | collective-permute-start | bytes 786440 | tf_op jit(solution)/shard_map/ppermute | solution.py:205
  105.0 2.5 %shard_map.67 = f32[2,4,256,128]{3,2,1,0:T(8,128)S(1)} custom-call(s32[2]{0:T(128)S(1)} %pad_add_fusion.refs_0_, bf16[1024,1024]{1,0:T(8,128)(2,1)S(1)} %copy-done, bf16[1024,1024]{1,0:T(8,128)(2,1)} %collective-permute-done.refs_2_, bf16[256,1024]{1,0:T(8,128)(2,1)S(1)} %shard_map.66.refs_3_), custom_call_target="tpu_custom_call" | custom-call | flops 21474836480 | bytes 4194304 | tf_op jit(solution)/shard_map/pallas_call | solution.py:186
  107.5 2.8 %collective-permute-done.9 = bf16[4,256,128]{2,1,0:T(8,128)(2,1)S(1)} collective-permute-done((bf16[4,256,128]{2,1,0:T(8,128)(2,1)S(1)}, bf16[4,256,128]{2,1,0:T(8,128)(2,1)S(1)}, u32[]{:S(2)}, u32[]{:S(2)}) %collective-permute-start.9) | collective-permute-done | bytes 262176 | tf_op jit(solution)/shard_map/ppermute | solution.py:205
  111.2 8.4 %all-to-all-start.1 = ((bf16[8,256,128]{2,1,0:T(8,128)(2,1)}), bf16[8,256,128]{2,1,0:T(8,128)(2,1)}, u32[]{:S(2)}, u32[]{:S(2)}) async-start(bf16[8,256,128]{2,1,0:T(8,128)(2,1)} %bitcast.35), calls=%async_computation.1 | async-start | bytes 1048576 | tf_op jit(solution)/shard_map/all_to_all | solution.py:220
  119.7 2.5 %shard_map.70 = (bf16[4,256,128]{2,1,0:T(8,128)(2,1)S(1)}, bf16[4,256,128]{2,1,0:T(8,128)(2,1)S(1)}) custom-call(s32[2]{0:T(128)S(1)} %pad_add_fusion.refs_0_, bf16[1024,1024]{1,0:T(8,128)(2,1)S(1)} %copy-done, bf16[1024,1024]{1,0:T(8,128)(2,1)} %collective-permute-done.refs_2_, bf16[256,1024]{1,0:T(8,128)(2,1)S(1)} %collective-permute-done.11.refs_3_), custom_call_target="tpu_custom_call" | custom-call | flops 21474836480 | bytes 4194304 | tf_op jit(solution)/shard_map/pallas_call | solution.py:186
  122.2 2.5 %collective-permute-start.12 = (bf16[4,256,128]{2,1,0:T(8,128)(2,1)S(1)}, bf16[4,256,128]{2,1,0:T(8,128)(2,1)S(1)}, u32[]{:S(2)}, u32[]{:S(2)}) collective-permute-start(bf16[4,256,128]{2,1,0:T(8,128)(2,1)S(1)} %get-tuple-element.27), channel_id=1, source_target_pairs={{0,1},{1,0},{2,3},{3,2},{4,5},{5,4},{6,7},{7,6},{8,9},{9,8},{10,11... | collective-permute-start | bytes 786440 | tf_op jit(solution)/shard_map/ppermute | solution.py:205
  124.7 5.1 %collective-permute-start.13 = (bf16[4,256,128]{2,1,0:T(8,128)(2,1)S(1)}, bf16[4,256,128]{2,1,0:T(8,128)(2,1)S(1)}, u32[]{:S(2)}, u32[]{:S(2)}) collective-permute-start(bf16[4,256,128]{2,1,0:T(8,128)(2,1)S(1)} %get-tuple-element.28), channel_id=1, source_target_pairs={{0,7},{1,2},{2,1},{3,4},{4,3},{5,6},{6,5},{7,0},{8,15},{9,10},{10,... | collective-permute-start | bytes 786440 | tf_op jit(solution)/shard_map/ppermute | solution.py:206
  129.8 2.5 %shard_map.69 = f32[2,4,256,128]{3,2,1,0:T(8,128)S(1)} custom-call(s32[2]{0:T(128)S(1)} %pad_add_fusion.refs_0_, bf16[1024,1024]{1,0:T(8,128)(2,1)S(1)} %copy-done, bf16[1024,1024]{1,0:T(8,128)(2,1)} %collective-permute-done.refs_2_, bf16[256,1024]{1,0:T(8,128)(2,1)S(1)} %collective-permute-done.11.refs_3_), custom_call_target="tpu_custom_call" | custom-call | flops 21474836480 | bytes 4194304 | tf_op jit(solution)/shard_map/pallas_call | solution.py:186
  132.3 6.1 %collective-permute-done.12 = bf16[4,256,128]{2,1,0:T(8,128)(2,1)S(1)} collective-permute-done((bf16[4,256,128]{2,1,0:T(8,128)(2,1)S(1)}, bf16[4,256,128]{2,1,0:T(8,128)(2,1)S(1)}, u32[]{:S(2)}, u32[]{:S(2)}) %collective-permute-start.12) | collective-permute-done | bytes 262176 | tf_op jit(solution)/shard_map/ppermute | solution.py:205
  138.4 2.0 %collective-permute-done.13 = bf16[4,256,128]{2,1,0:T(8,128)(2,1)S(1)} collective-permute-done((bf16[4,256,128]{2,1,0:T(8,128)(2,1)S(1)}, bf16[4,256,128]{2,1,0:T(8,128)(2,1)S(1)}, u32[]{:S(2)}, u32[]{:S(2)}) %collective-permute-start.13) | collective-permute-done | bytes 262176 | tf_op jit(solution)/shard_map/ppermute | solution.py:206
  141.4 5.0 %all-to-all-start.2 = ((bf16[8,256,128]{2,1,0:T(8,128)(2,1)}), bf16[8,256,128]{2,1,0:T(8,128)(2,1)S(1)}, u32[]{:S(2)}, u32[]{:S(2)}) async-start(bf16[8,256,128]{2,1,0:T(8,128)(2,1)} %bitcast.15), calls=%async_computation.2 | async-start | bytes 1048576 | tf_op jit(solution)/shard_map/all_to_all | solution.py:220
  146.4 1.1 reduce_sum.24
  147.6 13.2 %all-to-all-done.2 = bf16[8,256,128]{2,1,0:T(8,128)(2,1)S(1)} async-done(((bf16[8,256,128]{2,1,0:T(8,128)(2,1)}), bf16[8,256,128]{2,1,0:T(8,128)(2,1)S(1)}, u32[]{:S(2)}, u32[]{:S(2)}) %all-to-all-start.2) | async-done | bytes 524320 | tf_op jit(solution)/shard_map/all_to_all | solution.py:220
  (27 shorter events, 3.9 us)
Async XLA Ops:
  0.0 6.9 %copy-start = (bf16[1024,1024]{1,0:T(8,128)(2,1)S(1)}, bf16[1024,1024]{1,0:T(8,128)(2,1)}, u32[]{:S(2)}) copy-start(bf16[1024,1024]{1,0:T(8,128)(2,1)} %refs_1_.7) | copy-start | bytes 6291460
  0.0 70.9 %copy-start.1 = (bf16[1,256,1024]{2,1,0:T(8,128)(2,1)S(1)}, bf16[1,256,1024]{2,1,0:T(8,128)(2,1)}, u32[]{:S(2)}) copy-start(bf16[1,256,1024]{2,1,0:T(8,128)(2,1)} %param.8) | copy-start | bytes 1572868
  0.0 70.9 %copy-start.2 = (bf16[2,1,256,128]{3,2,1,0:T(8,128)(2,1)S(1)}, bf16[2,1,256,128]{3,2,1,0:T(8,128)(2,1)}, u32[]{:S(2)}) copy-start(bf16[2,1,256,128]{3,2,1,0:T(8,128)(2,1)} %param.9) | copy-start | bytes 393220
  0.0 32.2 %all-to-all-start = ((bf16[8,1024,128]{2,1,0:T(8,128)(2,1)}), bf16[8,1024,128]{2,1,0:T(8,128)(2,1)}, u32[]{:S(2)}, u32[]{:S(2)}) async-start(bf16[8,1024,128]{2,1,0:T(8,128)(2,1)} %bitcast.34), calls=%async_computation | async-start | bytes 4194304 | tf_op jit(solution)/shard_map/all_to_all | solution.py:152
  6.9 88.5 %collective-permute-start = (bf16[1024,1024]{1,0:T(8,128)(2,1)S(1)}, bf16[1024,1024]{1,0:T(8,128)(2,1)}, u32[]{:S(2)}, u32[]{:S(2)}) collective-permute-start(bf16[1024,1024]{1,0:T(8,128)(2,1)S(1)} %copy-done), channel_id=1, source_target_pairs={{0,8},{8,0},{16,24},{24,16},{1,9},{9,1},{17,25},{25,17},{2,10},{10... | collective-permute-start | bytes 6291464 | tf_op jit(solution)/shard_map/ppermute | solution.py:235
  33.2 18.3 %collective-permute-start.1 = (bf16[1024,128]{1,0:T(8,128)(2,1)S(1)}, bf16[1024,128]{1,0:T(8,128)(2,1)S(1)}, u32[]{:S(2)}, u32[]{:S(2)}) collective-permute-start(bf16[1024,128]{1,0:T(8,128)(2,1)S(1)} %dynamic-slice_bitcast_fusion), channel_id=1, source_target_pairs={{0,64},{32,96},{64,0},{96,32},{128,192},{160,224},{192,128},{224,1... | collective-permute-start | bytes 786440 | tf_op jit(solution)/shard_map/ppermute | solution.py:158
  52.4 9.3 %collective-permute-start.4 = (bf16[1024,128]{1,0:T(8,128)(2,1)S(1)}, bf16[1024,128]{1,0:T(8,128)(2,1)S(1)}, u32[]{:S(2)}, u32[]{:S(2)}) collective-permute-start(bf16[1024,128]{1,0:T(8,128)(2,1)S(1)} %broadcast_select_fusion.refs_2_), channel_id=1, source_target_pairs={{0,32},{32,0},{64,96},{96,64},{128,160},{160,128},{192,224},{224,1... | collective-permute-start | bytes 786440 | tf_op jit(solution)/shard_map/ppermute | solution.py:248
  55.7 12.6 %collective-permute-start.2 = (bf16[1024,128]{1,0:T(8,128)(2,1)S(1)}, bf16[1024,128]{1,0:T(8,128)(2,1)S(1)}, u32[]{:S(2)}, u32[]{:S(2)}) collective-permute-start(bf16[1024,128]{1,0:T(8,128)(2,1)S(1)} %broadcast_select_fusion.refs_2_), channel_id=1, source_target_pairs={{0,384},{32,416},{64,448},{96,480},{128,0},{160,32},{192,64},{224,... | collective-permute-start | bytes 786440 | tf_op jit(solution)/shard_map/ppermute | solution.py:239
  59.0 18.6 %collective-permute-start.7 = (bf16[1024,128]{1,0:T(8,128)(2,1)S(1)}, bf16[1024,128]{1,0:T(8,128)(2,1)}, u32[]{:S(2)}, u32[]{:S(2)}) collective-permute-start(bf16[1024,128]{1,0:T(8,128)(2,1)S(1)} %broadcast_select_fusion.refs_2_), channel_id=1, source_target_pairs={{0,128},{32,160},{64,192},{96,224},{128,256},{160,288},{192,320},{... | collective-permute-start | bytes 786440 | tf_op jit(solution)/shard_map/ppermute | solution.py:239
  61.7 13.0 %collective-permute-start.5 = (bf16[1024,128]{1,0:T(8,128)(2,1)S(1)}, bf16[1024,128]{1,0:T(8,128)(2,1)}, u32[]{:S(2)}, u32[]{:S(2)}) collective-permute-start(bf16[1024,128]{1,0:T(8,128)(2,1)S(1)} %collective-permute-done.4.refs_3_), channel_id=1, source_target_pairs={{0,128},{32,160},{64,192},{96,224},{128,256},{160,288},{192,320},{... | collective-permute-start | bytes 786440 | tf_op jit(solution)/shard_map/ppermute | solution.py:239
  63.7 14.0 %collective-permute-start.8 = (bf16[1024,128]{1,0:T(8,128)(2,1)S(1)}, bf16[1024,128]{1,0:T(8,128)(2,1)}, u32[]{:S(2)}, u32[]{:S(2)}) collective-permute-start(bf16[1024,128]{1,0:T(8,128)(2,1)S(1)} %collective-permute-done.4.refs_3_), channel_id=1, source_target_pairs={{0,384},{32,416},{64,448},{96,480},{128,0},{160,32},{192,64},{224,... | collective-permute-start | bytes 786440 | tf_op jit(solution)/shard_map/ppermute | solution.py:239
  68.3 15.7 %collective-permute-start.3 = (bf16[1024,128]{1,0:T(8,128)(2,1)S(1)}, bf16[1024,128]{1,0:T(8,128)(2,1)S(1)}, u32[]{:S(2)}, u32[]{:S(2)}) collective-permute-start(bf16[1024,128]{1,0:T(8,128)(2,1)S(1)} %collective-permute-done.2.refs_4_), channel_id=1, source_target_pairs={{0,384},{32,416},{64,448},{96,480},{128,0},{160,32},{192,64},{224,... | collective-permute-start | bytes 786440 | tf_op jit(solution)/shard_map/ppermute | solution.py:239
  74.7 9.3 %collective-permute-start.6 = (bf16[1024,128]{1,0:T(8,128)(2,1)}, bf16[1024,128]{1,0:T(8,128)(2,1)S(1)}, u32[]{:S(2)}, u32[]{:S(2)}) collective-permute-start(bf16[1024,128]{1,0:T(8,128)(2,1)} %collective-permute-done.5.refs_3_), channel_id=1, source_target_pairs={{0,128},{32,160},{64,192},{96,224},{128,256},{160,288},{192,320},{... | collective-permute-start | bytes 786440 | tf_op jit(solution)/shard_map/ppermute | solution.py:239
  87.5 32.2 %collective-permute-start.11 = (bf16[256,1024]{1,0:T(8,128)(2,1)S(1)}, bf16[256,1024]{1,0:T(8,128)(2,1)S(1)}, u32[]{:S(2)}, u32[]{:S(2)}) collective-permute-start(bf16[256,1024]{1,0:T(8,128)(2,1)S(1)} %shard_map.66.refs_3_), channel_id=1, source_target_pairs={{0,16},{8,24},{16,0},{24,8},{1,17},{9,25},{17,1},{25,9},{2,18},{10... | collective-permute-start | bytes 1572872 | tf_op jit(solution)/shard_map/ppermute | solution.py:235
  98.0 9.6 %collective-permute-start.10 = (bf16[4,256,128]{2,1,0:T(8,128)(2,1)S(1)}, bf16[4,256,128]{2,1,0:T(8,128)(2,1)S(1)}, u32[]{:S(2)}, u32[]{:S(2)}) collective-permute-start(bf16[4,256,128]{2,1,0:T(8,128)(2,1)S(1)} %get-tuple-element.25), channel_id=1, source_target_pairs={{0,7},{1,2},{2,1},{3,4},{4,3},{5,6},{6,5},{7,0},{8,15},{9,10},{10,... | collective-permute-start | bytes 786440 | tf_op jit(solution)/shard_map/ppermute | solution.py:206
  103.1 7.2 %collective-permute-start.9 = (bf16[4,256,128]{2,1,0:T(8,128)(2,1)S(1)}, bf16[4,256,128]{2,1,0:T(8,128)(2,1)S(1)}, u32[]{:S(2)}, u32[]{:S(2)}) collective-permute-start(bf16[4,256,128]{2,1,0:T(8,128)(2,1)S(1)} %get-tuple-element.24), channel_id=1, source_target_pairs={{0,1},{1,0},{2,3},{3,2},{4,5},{5,4},{6,7},{7,6},{8,9},{9,8},{10,11... | collective-permute-start | bytes 786440 | tf_op jit(solution)/shard_map/ppermute | solution.py:205
  111.2 30.2 %all-to-all-start.1 = ((bf16[8,256,128]{2,1,0:T(8,128)(2,1)}), bf16[8,256,128]{2,1,0:T(8,128)(2,1)}, u32[]{:S(2)}, u32[]{:S(2)}) async-start(bf16[8,256,128]{2,1,0:T(8,128)(2,1)} %bitcast.35), calls=%async_computation.1 | async-start | bytes 1048576 | tf_op jit(solution)/shard_map/all_to_all | solution.py:220
  122.2 16.3 %collective-permute-start.12 = (bf16[4,256,128]{2,1,0:T(8,128)(2,1)S(1)}, bf16[4,256,128]{2,1,0:T(8,128)(2,1)S(1)}, u32[]{:S(2)}, u32[]{:S(2)}) collective-permute-start(bf16[4,256,128]{2,1,0:T(8,128)(2,1)S(1)} %get-tuple-element.27), channel_id=1, source_target_pairs={{0,1},{1,0},{2,3},{3,2},{4,5},{5,4},{6,7},{7,6},{8,9},{9,8},{10,11... | collective-permute-start | bytes 786440 | tf_op jit(solution)/shard_map/ppermute | solution.py:205
  124.7 15.8 %collective-permute-start.13 = (bf16[4,256,128]{2,1,0:T(8,128)(2,1)S(1)}, bf16[4,256,128]{2,1,0:T(8,128)(2,1)S(1)}, u32[]{:S(2)}, u32[]{:S(2)}) collective-permute-start(bf16[4,256,128]{2,1,0:T(8,128)(2,1)S(1)} %get-tuple-element.28), channel_id=1, source_target_pairs={{0,7},{1,2},{2,1},{3,4},{4,3},{5,6},{6,5},{7,0},{8,15},{9,10},{10,... | collective-permute-start | bytes 786440 | tf_op jit(solution)/shard_map/ppermute | solution.py:206
  141.4 19.4 %all-to-all-start.2 = ((bf16[8,256,128]{2,1,0:T(8,128)(2,1)}), bf16[8,256,128]{2,1,0:T(8,128)(2,1)S(1)}, u32[]{:S(2)}, u32[]{:S(2)}) async-start(bf16[8,256,128]{2,1,0:T(8,128)(2,1)} %bitcast.15), calls=%async_computation.2 | async-start | bytes 1048576 | tf_op jit(solution)/shard_map/all_to_all | solution.py:220

commit v4 on v3

--- a/solution.py
+++ b/solution.py
@@ -144,7 +144,7 @@
     return out[0] if last else out
 
 
-def spread_piece(prompt_kv, owner):
+def spread_piece(prompt_kv, owner, ready):
     me = lax.axis_index("cand")
     z = me % NZ
     owner_x, owner_z = owner // NZ, owner % NZ
@@ -156,16 +156,35 @@
         arrived, (owner_z % 2) * NX + owner_x, axis=0, keepdims=False
     )
     crossed = lax.ppermute(piece, "cand", cand_pairs(lambda x, z: (x, z ^ 2)))
-    return jnp.where(owner_z // 2 == z // 2, piece, crossed)
-
-
-def projection_kernel(kept, place_ref, own_ref, other_ref, rows_ref, *out_refs):
+    crossed, ready = lax.optimization_barrier((crossed, ready))
+    return jnp.where(owner_z // 2 == z // 2, piece, crossed), ready
+
+
+def interleave_kernel(own_ref, other_ref, out_ref):
+    for i in range(own_ref.shape[1] // HD):
+        out_ref[:, 2 * i * HD : (2 * i + 1) * HD] = own_ref[:, i * HD : (i + 1) * HD]
+        out_ref[:, (2 * i + 1) * HD : (2 * i + 2) * HD] = other_ref[:, i * HD : (i + 1) * HD]
+
+
+def interleave(own, other):
+    vmem = pl.BlockSpec(memory_space=pltpu.VMEM)
+    return pl.pallas_call(
+        interleave_kernel,
+        out_shape=jax.ShapeDtypeStruct((own.shape[0], 2 * own.shape[1]), own.dtype),
+        in_specs=[vmem] * 2,
+        out_specs=vmem,
+        compiler_params=pltpu.CompilerParams(vmem_limit_bytes=16 * 1024 * 1024),
+        cost_estimate=pl.CostEstimate(flops=0, bytes_accessed=8 * own.size, transcendentals=0),
+    )(own, other)
+
+
+def projection_kernel(kept, place_ref, weight_ref, rows_ref, *out_refs):
     rows = rows_ref[...]
     core, parity = place_ref[0], place_ref[1]
-    for j in range(own_ref.shape[1] // HD // 2):
+    for j in range(weight_ref.shape[1] // HD // 4):
         block = 2 * j + (parity if kept else 1 - parity)
-        lanes = pl.ds(pl.multiple_of(block * HD, HD), HD)
-        both = dot_n(rows, jnp.concatenate([own_ref[:, lanes], other_ref[:, lanes]], axis=1))
+        lanes = pl.ds(pl.multiple_of(block * 2 * HD, 2 * HD), 2 * HD)
+        both = dot_n(rows, weight_ref[:, lanes])
         if kept:
             out_refs[0][core, j] = both[:, :HD]
             out_refs[0][1 - core, j] = both[:, HD:]
@@ -174,7 +193,7 @@
             out_refs[1][j] = both[:, HD:].astype(jnp.bfloat16)
 
 
-def project(rows, own, other, kept):
+def project(rows, weight, kept):
     n = lax.axis_size("tensor") // 2
     count, depth = rows.shape
     place = jnp.stack([lax.axis_index("prompt") % 2, lax.axis_index("tensor") % 2])
@@ -186,25 +205,25 @@
     return pl.pallas_call(
         lambda *refs: projection_kernel(kept, *refs),
         out_shape=out_shape,
-        in_specs=[pl.BlockSpec(memory_space=pltpu.SMEM)] + [vmem] * 3,
+        in_specs=[pl.BlockSpec(memory_space=pltpu.SMEM)] + [vmem] * 2,
         out_specs=[vmem] * len(out_shape),
         compiler_params=pltpu.CompilerParams(vmem_limit_bytes=32 * 1024 * 1024),
         cost_estimate=pl.CostEstimate(
-            flops=80 * own.shape[1] * count * depth,
-            bytes_accessed=4 * own.size,
+            flops=40 * weight.shape[1] * count * depth,
+            bytes_accessed=2 * weight.size,
             transcendentals=0,
         ),
-    )(place.astype(jnp.int32), own, other, rows)
-
-
-def pair_sums(rows, own, other):
-    own_sent, other_sent = project(rows, own, other, kept=False)
+    )(place.astype(jnp.int32), weight, rows)
+
+
+def pair_sums(rows, weight):
+    own_sent, other_sent = project(rows, weight, kept=False)
     n = lax.axis_size("tensor")
     up = [(t, (t + 1) % n if t % 2 == 0 else t - 1) for t in range(n)]
     down = [(t, (t - 1) % n if t % 2 == 0 else (t + 1) % n) for t in range(n)]
     own_got = lax.ppermute(own_sent, "tensor", up)
     other_got = lax.ppermute(other_sent, "tensor", down)
-    (keep,) = project(rows, own, other, kept=True)
+    (keep,) = project(rows, weight, kept=True)
     even = lax.axis_index("prompt") % 2 == 0
     got = [jnp.where(even, own_got, other_got), jnp.where(even, other_got, own_got)]
     return keep + jnp.stack(got).astype(jnp.float32)
@@ -241,8 +260,8 @@
 
 def body(owner_index, suffix_lengths, queries, suffix_kv, prompt_cache, out_weight):
     query_rows = queries[0]
-    weights = [out_weight, swap(out_weight, 1)]
-    piece = spread_piece(prompt_cache[:, 0, 0], owner_index[0])
+    weight = interleave(out_weight, swap(out_weight, 1))
+    piece, weight = spread_piece(prompt_cache[:, 0, 0], owner_index[0], weight)
     keys_first = (lax.axis_index("cand") % 2 == 0).astype(jnp.int32)
     scalars = jnp.stack([keys_first, suffix_lengths[0, 0]])
     other = lax.ppermute(piece, "cand", cand_pairs(lambda x, z: (x, z ^ 1)))
@@ -254,10 +273,10 @@
     state = attend(scalars, query_rows, [left, right], state=state)
     attended = attend(scalars, query_rows, [across], state=state, last=True)
     far_rows = swap(attended, 2)
-    near_terms = pair_sums(attended, *weights)
+    near_terms = pair_sums(attended, weight)
     near = exchange(near_terms)
     _, far_rows = lax.optimization_barrier((near_terms, far_rows))
-    far_terms, near = lax.optimization_barrier((pair_sums(far_rows, *weights), near))
+    far_terms, near = lax.optimization_barrier((pair_sums(far_rows, weight), near))
     far = add_up(exchange(far_terms))
     near = add_up(near)
     first = lax.axis_index("prompt") < 2

time: 164 us -> 162 us (0.988)
  local copies, waits for them, and re-layouts: 0.98 us -> 5.12 us
  Pallas kernels: 23.7 us -> 21 us
  waiting for transfers between devices: 53.6 us -> 51.6 us
    pallas_call x4, Pallas kernels: 10.1 us -> 5.23 us  [project(): pl.pallas_call(lambda *refs: projection_kernel(kept, *refs), out_shape=ou...]
    ppermute x1, waiting for transfers between devices: 11.4 us -> 6.73 us  [spread_piece(): crossed = lax.ppermute(piece, 'cand', cand_pairs(lambda x, z: (x, z ^ 2)))]
    unnamed x6 -> x12, local copies, waits for them, and re-layouts: 0.01 us -> 4.15 us
    pallas_call x0 -> x1, Pallas kernels: none -> 2.68 us  [interleave(): pl.pallas_call(interleave_kernel, out_shape=jax.ShapeDtypeStruct((own.sha...]
  transfers between devices with their start and end apart: 17 -> 17, of which waited for: 6 -> 7; matrix products, arithmetic and copies ran while one was open for 3% -> 2% of each run, Pallas kernels for 15% -> 11%
where the time goes in v4:
time: 162 us; the launch traced here: 160 us
  starting transfers between devices  76.5 us (47%)
  waiting for transfers between devices  51.6 us (32%)
  Pallas kernels  21 us (13%)
  local copies, waits for them, and re-layouts  5.12 us (3%)
  other arithmetic  3.95 us (2%)
  between operations  1.76 us (1%)
    all_to_all x1, waiting for transfers between devices, spread_piece(): lax.all_to_all(pieces, 'cand', split_axis=0, concat_axis=0, axis_index_gr...  18 us
    ppermute x6, starting transfers between devices, move(): return lax.ppermute(value, 'cand', cand_pairs(lambda x, z: (x + shift, z)))  17.2 us
    ppermute x2, starting transfers between devices, swap(): return lax.ppermute(value, 'prompt', [(p, p ^ bit) for p in range(4)])  14.4 us
    all_to_all x2, waiting for transfers between devices, exchange(): lax.all_to_all(terms.astype(jnp.bfloat16).reshape(cores * n, rows, column...  14.1 us
    all_to_all x2, starting transfers between devices, exchange(): lax.all_to_all(terms.astype(jnp.bfloat16).reshape(cores * n, rows, column...  13.4 us
    pallas_call x3, Pallas kernels, attend(): pl.pallas_call(lambda *refs: attention_kernel(len(blocks), suffix is not...  13.1 us
    ppermute x2, starting transfers between devices, pair_sums(): other_got = lax.ppermute(other_sent, 'tensor', down)  10.1 us
    ppermute x2, waiting for transfers between devices, pair_sums(): own_got = lax.ppermute(own_sent, 'tensor', up)  9.73 us
  transfers between devices with their start and end apart: 17, of which 7 were waited for; matrix products, arithmetic and copies ran while one was open for 2% of the time, Pallas kernels for 11%

profile of v4, /device:TPU:1, one launch (start us, length us, event | category | flops | bytes accessed | tf_op | source)
XLA Modules:
  0.0 159.9 jit_solution(1831156714951014030)
XLA Ops:
  0.0 6.8 %all-to-all-start = ((bf16[8,1024,128]{2,1,0:T(8,128)(2,1)}), bf16[8,1024,128]{2,1,0:T(8,128)(2,1)}, u32[]{:S(2)}, u32[]{:S(2)}) async-start(bf16[8,1024,128]{2,1,0:T(8,128)(2,1)} %bitcast.34), calls=%async_computation | async-start | bytes 4194304 | tf_op jit(solution)/shard_map/all_to_all | solution.py:152
  6.8 6.5 %collective-permute-start.1 = (bf16[1024,1024]{1,0:T(8,128)(2,1)S(1)}, bf16[1024,1024]{1,0:T(8,128)(2,1)}, u32[]{:S(2)}, u32[]{:S(2)}) collective-permute-start(bf16[1024,1024]{1,0:T(8,128)(2,1)S(1)} %copy-done.3), channel_id=1, source_target_pairs={{0,8},{8,0},{16,24},{24,16},{1,9},{9,1},{17,25},{25,17},{2,10},{10... | collective-permute-start | bytes 6291464 | tf_op jit(solution)/shard_map/ppermute | solution.py:254
  14.0 18.0 %all-to-all-done = bf16[8,1024,128]{2,1,0:T(8,128)(2,1)} async-done(((bf16[8,1024,128]{2,1,0:T(8,128)(2,1)}), bf16[8,1024,128]{2,1,0:T(8,128)(2,1)}, u32[]{:S(2)}, u32[]{:S(2)}) %all-to-all-start) | async-done | bytes 2097184 | tf_op jit(solution)/shard_map/all_to_all | solution.py:152
  33.0 6.8 %collective-permute-start = (bf16[1024,128]{1,0:T(8,128)(2,1)S(1)}, bf16[1024,128]{1,0:T(8,128)(2,1)S(1)}, u32[]{:S(2)}, u32[]{:S(2)}) collective-permute-start(bf16[1024,128]{1,0:T(8,128)(2,1)S(1)} %dynamic-slice_bitcast_fusion), channel_id=1, source_target_pairs={{0,64},{32,96},{64,0},{96,32},{128,192},{160,224},{192,128},{224,1... | collective-permute-start | bytes 786440 | tf_op jit(solution)/shard_map/ppermute | solution.py:158
  39.9 2.7 %shard_map.64.refs_1_ = bf16[1024,2048]{1,0:T(8,128)(2,1)S(1)} custom-call(bf16[1024,1024]{1,0:T(8,128)(2,1)S(1)} %copy-done.3, bf16[1024,1024]{1,0:T(8,128)(2,1)} %collective-permute-done.1.other_ref), custom_call_target="tpu_custom_call" | custom-call | bytes 8388608 | tf_op jit(solution)/shard_map/pallas_call | solution.py:171
  42.6 1.9 %copy-done = bf16[1024,2048]{1,0:T(8,128)(2,1)} copy-done((bf16[1024,2048]{1,0:T(8,128)(2,1)}, bf16[1024,2048]{1,0:T(8,128)(2,1)S(1)}, u32[]{:S(2)}) %copy-start) | copy-done | bytes 4194328
  44.6 6.7 %collective-permute-done = bf16[1024,128]{1,0:T(8,128)(2,1)S(1)} collective-permute-done((bf16[1024,128]{1,0:T(8,128)(2,1)S(1)}, bf16[1024,128]{1,0:T(8,128)(2,1)S(1)}, u32[]{:S(2)}, u32[]{:S(2)}) %collective-permute-start) | collective-permute-done | bytes 262176 | tf_op jit(solution)/shard_map/ppermute | solution.py:158
  52.3 3.2 %collective-permute-start.4 = (bf16[1024,128]{1,0:T(8,128)(2,1)S(1)}, bf16[1024,128]{1,0:T(8,128)(2,1)S(1)}, u32[]{:S(2)}, u32[]{:S(2)}) collective-permute-start(bf16[1024,128]{1,0:T(8,128)(2,1)S(1)} %broadcast_select_fusion.refs_2_), channel_id=1, source_target_pairs={{0,32},{32,0},{64,96},{96,64},{128,160},{160,128},{192,224},{224,1... | collective-permute-start | bytes 786440 | tf_op jit(solution)/shard_map/ppermute | solution.py:267
  55.5 2.6 %collective-permute-start.2 = (bf16[1024,128]{1,0:T(8,128)(2,1)S(1)}, bf16[1024,128]{1,0:T(8,128)(2,1)S(1)}, u32[]{:S(2)}, u32[]{:S(2)}) collective-permute-start(bf16[1024,128]{1,0:T(8,128)(2,1)S(1)} %broadcast_select_fusion.refs_2_), channel_id=1, source_target_pairs={{0,384},{32,416},{64,448},{96,480},{128,0},{160,32},{192,64},{224,... | collective-permute-start | bytes 786440 | tf_op jit(solution)/shard_map/ppermute | solution.py:258
  58.9 2.7 %collective-permute-start.7 = (bf16[1024,128]{1,0:T(8,128)(2,1)S(1)}, bf16[1024,128]{1,0:T(8,128)(2,1)S(1)}, u32[]{:S(2)}, u32[]{:S(2)}) collective-permute-start(bf16[1024,128]{1,0:T(8,128)(2,1)S(1)} %broadcast_select_fusion.refs_2_), channel_id=1, source_target_pairs={{0,128},{32,160},{64,192},{96,224},{128,256},{160,288},{192,320},{... | collective-permute-start | bytes 786440 | tf_op jit(solution)/shard_map/ppermute | solution.py:258
  61.6 1.9 %collective-permute-start.5 = (bf16[1024,128]{1,0:T(8,128)(2,1)S(1)}, bf16[1024,128]{1,0:T(8,128)(2,1)S(1)}, u32[]{:S(2)}, u32[]{:S(2)}) collective-permute-start(bf16[1024,128]{1,0:T(8,128)(2,1)S(1)} %collective-permute-done.4.refs_3_), channel_id=1, source_target_pairs={{0,128},{32,160},{64,192},{96,224},{128,256},{160,288},{192,320},{... | collective-permute-start | bytes 786440 | tf_op jit(solution)/shard_map/ppermute | solution.py:258
  63.5 4.6 %collective-permute-start.8 = (bf16[1024,128]{1,0:T(8,128)(2,1)S(1)}, bf16[1024,128]{1,0:T(8,128)(2,1)S(1)}, u32[]{:S(2)}, u32[]{:S(2)}) collective-permute-start(bf16[1024,128]{1,0:T(8,128)(2,1)S(1)} %collective-permute-done.4.refs_3_), channel_id=1, source_target_pairs={{0,384},{32,416},{64,448},{96,480},{128,0},{160,32},{192,64},{224,... | collective-permute-start | bytes 786440 | tf_op jit(solution)/shard_map/ppermute | solution.py:258
  68.2 2.5 %collective-permute-start.3 = (bf16[1024,128]{1,0:T(8,128)(2,1)S(1)}, bf16[1024,128]{1,0:T(8,128)(2,1)S(1)}, u32[]{:S(2)}, u32[]{:S(2)}) collective-permute-start(bf16[1024,128]{1,0:T(8,128)(2,1)S(1)} %collective-permute-done.2.refs_4_), channel_id=1, source_target_pairs={{0,384},{32,416},{64,448},{96,480},{128,0},{160,32},{192,64},{224,... | collective-permute-start | bytes 786440 | tf_op jit(solution)/shard_map/ppermute | solution.py:258
  70.8 3.8 %shard_map.65 = (f32[256,1024]{1,0:T(8,128)S(1)}, f32[256,1024]{1,0:T(8,128)S(1)}, f32[256,1024]{1,0:T(8,128)S(1)}) custom-call(s32[2]{0:T(128)S(1)} %pad_add_fusion.1.refs_0_, bf16[256,1024]{1,0:T(8,128)(2,1)S(1)} %bitcast.30, bf16[1024,128]{1,0:T(8,128)(2,1)S(1)} %broadcast_select_fusion.refs_2_, bf16[1024,128]{1,0:T(8,128)(2,1)S(1)} %collective-permute-done.4.refs_3_, ...), custom_call_target="tpu_custom_call" | custom-call | flops 2684354560 | bytes 4194304 | tf_op jit(solution)/shard_map/pallas_call | solution.py:130
  74.6 2.9 %collective-permute-start.6 = (bf16[1024,128]{1,0:T(8,128)(2,1)S(1)}, bf16[1024,128]{1,0:T(8,128)(2,1)S(1)}, u32[]{:S(2)}, u32[]{:S(2)}) collective-permute-start(bf16[1024,128]{1,0:T(8,128)(2,1)S(1)} %collective-permute-done.5.refs_3_), channel_id=1, source_target_pairs={{0,128},{32,160},{64,192},{96,224},{128,256},{160,288},{192,320},{... | collective-permute-start | bytes 786440 | tf_op jit(solution)/shard_map/ppermute | solution.py:258
  77.5 5.8 %shard_map.66 = (f32[256,1024]{1,0:T(8,128)S(1)}, f32[256,1024]{1,0:T(8,128)S(1)}, f32[256,1024]{1,0:T(8,128)S(1)}) custom-call(s32[2]{0:T(128)S(1)} %pad_add_fusion.1.refs_0_, bf16[256,1024]{1,0:T(8,128)(2,1)S(1)} %bitcast.31, bf16[1024,128]{1,0:T(8,128)(2,1)S(1)} %collective-permute-done.7.refs_2_, bf16[1024,128]{1,0:T(8,128)(2,1)S(1)} %collective-permute-done.5.refs_3_, ...), custom_call_target="tpu_custom_call" | custom-call | flops 4294967296 | bytes 4194304 | tf_op jit(solution)/shard_map/pallas_call | solution.py:130
  83.4 3.5 %shard_map.67.refs_2_ = bf16[256,1024]{1,0:T(8,128)(2,1)S(1)} custom-call(s32[2]{0:T(128)S(1)} %pad_add_fusion.1.refs_0_, bf16[256,1024]{1,0:T(8,128)(2,1)S(1)} %bitcast.32, bf16[1024,128]{1,0:T(8,128)(2,1)S(1)} %collective-permute-done.3.refs_2_, bf16[1024,128]{1,0:T(8,128)(2,1)S(1)} %collective-permute-done.6.refs_3_, ...), custom_call_target="tpu_custom_call" | custom-call | flops 2147483648 | bytes 4194304 | tf_op jit(solution)/shard_map/pallas_call | solution.py:130
  86.8 7.9 %collective-permute-start.11 = (bf16[256,1024]{1,0:T(8,128)(2,1)S(1)}, bf16[256,1024]{1,0:T(8,128)(2,1)S(1)}, u32[]{:S(2)}, u32[]{:S(2)}) collective-permute-start(bf16[256,1024]{1,0:T(8,128)(2,1)S(1)} %shard_map.67.refs_2_), channel_id=1, source_target_pairs={{0,16},{8,24},{16,0},{24,8},{1,17},{9,25},{17,1},{25,9},{2,18},{10... | collective-permute-start | bytes 1572872 | tf_op jit(solution)/shard_map/ppermute | solution.py:254
  94.8 1.3 shard_map.69
  96.1 5.1 %collective-permute-start.10 = (bf16[4,256,128]{2,1,0:T(8,128)(2,1)S(1)}, bf16[4,256,128]{2,1,0:T(8,128)(2,1)S(1)}, u32[]{:S(2)}, u32[]{:S(2)}) collective-permute-start(bf16[4,256,128]{2,1,0:T(8,128)(2,1)S(1)} %get-tuple-element.29), channel_id=1, source_target_pairs={{0,7},{1,2},{2,1},{3,4},{4,3},{5,6},{6,5},{7,0},{8,15},{9,10},{10,... | collective-permute-start | bytes 786440 | tf_op jit(solution)/shard_map/ppermute | solution.py:225
  101.2 1.9 %collective-permute-start.9 = (bf16[4,256,128]{2,1,0:T(8,128)(2,1)S(1)}, bf16[4,256,128]{2,1,0:T(8,128)(2,1)S(1)}, u32[]{:S(2)}, u32[]{:S(2)}) collective-permute-start(bf16[4,256,128]{2,1,0:T(8,128)(2,1)S(1)} %get-tuple-element.28), channel_id=1, source_target_pairs={{0,1},{1,0},{2,3},{3,2},{4,5},{5,4},{6,7},{7,6},{8,9},{9,8},{10,11... | collective-permute-start | bytes 786440 | tf_op jit(solution)/shard_map/ppermute | solution.py:224
  103.1 1.3 shard_map.68
  105.2 3.4 %collective-permute-done.9 = bf16[4,256,128]{2,1,0:T(8,128)(2,1)S(1)} collective-permute-done((bf16[4,256,128]{2,1,0:T(8,128)(2,1)S(1)}, bf16[4,256,128]{2,1,0:T(8,128)(2,1)S(1)}, u32[]{:S(2)}, u32[]{:S(2)}) %collective-permute-start.9) | collective-permute-done | bytes 262176 | tf_op jit(solution)/shard_map/ppermute | solution.py:224
  109.6 8.5 %all-to-all-start.1 = ((bf16[8,256,128]{2,1,0:T(8,128)(2,1)}), bf16[8,256,128]{2,1,0:T(8,128)(2,1)S(1)}, u32[]{:S(2)}, u32[]{:S(2)}) async-start(bf16[8,256,128]{2,1,0:T(8,128)(2,1)} %bitcast.13), calls=%async_computation.1 | async-start | bytes 1048576 | tf_op jit(solution)/shard_map/all_to_all | solution.py:239
  118.1 2.2 %copy-done.2 = bf16[1024,2048]{1,0:T(8,128)(2,1)S(1)} copy-done((bf16[1024,2048]{1,0:T(8,128)(2,1)S(1)}, bf16[1024,2048]{1,0:T(8,128)(2,1)}, u32[]{:S(2)}) %copy-start.2) | copy-done | bytes 4194328
  121.6 2.6 %collective-permute-start.12 = (bf16[4,256,128]{2,1,0:T(8,128)(2,1)S(1)}, bf16[4,256,128]{2,1,0:T(8,128)(2,1)S(1)}, u32[]{:S(2)}, u32[]{:S(2)}) collective-permute-start(bf16[4,256,128]{2,1,0:T(8,128)(2,1)S(1)} %get-tuple-element.31), channel_id=1, source_target_pairs={{0,1},{1,0},{2,3},{3,2},{4,5},{5,4},{6,7},{7,6},{8,9},{9,8},{10,11... | collective-permute-start | bytes 786440 | tf_op jit(solution)/shard_map/ppermute | solution.py:224
  124.1 5.1 %collective-permute-start.13 = (bf16[4,256,128]{2,1,0:T(8,128)(2,1)S(1)}, bf16[4,256,128]{2,1,0:T(8,128)(2,1)S(1)}, u32[]{:S(2)}, u32[]{:S(2)}) collective-permute-start(bf16[4,256,128]{2,1,0:T(8,128)(2,1)S(1)} %get-tuple-element.32), channel_id=1, source_target_pairs={{0,7},{1,2},{2,1},{3,4},{4,3},{5,6},{6,5},{7,0},{8,15},{9,10},{10,... | collective-permute-start | bytes 786440 | tf_op jit(solution)/shard_map/ppermute | solution.py:225
  129.2 1.3 shard_map.70
  130.5 6.4 %collective-permute-done.12 = bf16[4,256,128]{2,1,0:T(8,128)(2,1)S(1)} collective-permute-done((bf16[4,256,128]{2,1,0:T(8,128)(2,1)S(1)}, bf16[4,256,128]{2,1,0:T(8,128)(2,1)S(1)}, u32[]{:S(2)}, u32[]{:S(2)}) %collective-permute-start.12) | collective-permute-done | bytes 262176 | tf_op jit(solution)/shard_map/ppermute | solution.py:224
  136.9 2.2 %collective-permute-done.13 = bf16[4,256,128]{2,1,0:T(8,128)(2,1)S(1)} collective-permute-done((bf16[4,256,128]{2,1,0:T(8,128)(2,1)S(1)}, bf16[4,256,128]{2,1,0:T(8,128)(2,1)S(1)}, u32[]{:S(2)}, u32[]{:S(2)}) %collective-permute-start.13) | collective-permute-done | bytes 262176 | tf_op jit(solution)/shard_map/ppermute | solution.py:225
  140.0 4.8 %all-to-all-start.2 = ((bf16[8,256,128]{2,1,0:T(8,128)(2,1)}), bf16[8,256,128]{2,1,0:T(8,128)(2,1)S(1)}, u32[]{:S(2)}, u32[]{:S(2)}) async-start(bf16[8,256,128]{2,1,0:T(8,128)(2,1)} %bitcast.15), calls=%async_computation.2 | async-start | bytes 1048576 | tf_op jit(solution)/shard_map/all_to_all | solution.py:239
  145.0 14.1 %all-to-all-done.2 = bf16[8,256,128]{2,1,0:T(8,128)(2,1)S(1)} async-done(((bf16[8,256,128]{2,1,0:T(8,128)(2,1)}), bf16[8,256,128]{2,1,0:T(8,128)(2,1)S(1)}, u32[]{:S(2)}, u32[]{:S(2)}) %all-to-all-start.2) | async-done | bytes 524320 | tf_op jit(solution)/shard_map/all_to_all | solution.py:239
  (34 shorter events, 7.0 us)
Async XLA Ops:
  0.0 6.8 %copy-start.3 = (bf16[1024,1024]{1,0:T(8,128)(2,1)S(1)}, bf16[1024,1024]{1,0:T(8,128)(2,1)}, u32[]{:S(2)}) copy-start(bf16[1024,1024]{1,0:T(8,128)(2,1)} %own_ref.1) | copy-start | bytes 6291460
  0.0 32.0 %all-to-all-start = ((bf16[8,1024,128]{2,1,0:T(8,128)(2,1)}), bf16[8,1024,128]{2,1,0:T(8,128)(2,1)}, u32[]{:S(2)}, u32[]{:S(2)}) async-start(bf16[8,1024,128]{2,1,0:T(8,128)(2,1)} %bitcast.34), calls=%async_computation | async-start | bytes 4194304 | tf_op jit(solution)/shard_map/all_to_all | solution.py:152
  6.8 33.1 %collective-permute-start.1 = (bf16[1024,1024]{1,0:T(8,128)(2,1)S(1)}, bf16[1024,1024]{1,0:T(8,128)(2,1)}, u32[]{:S(2)}, u32[]{:S(2)}) collective-permute-start(bf16[1024,1024]{1,0:T(8,128)(2,1)S(1)} %copy-done.3), channel_id=1, source_target_pairs={{0,8},{8,0},{16,24},{24,16},{1,9},{9,1},{17,25},{25,17},{2,10},{10... | collective-permute-start | bytes 6291464 | tf_op jit(solution)/shard_map/ppermute | solution.py:254
  33.0 18.3 %collective-permute-start = (bf16[1024,128]{1,0:T(8,128)(2,1)S(1)}, bf16[1024,128]{1,0:T(8,128)(2,1)S(1)}, u32[]{:S(2)}, u32[]{:S(2)}) collective-permute-start(bf16[1024,128]{1,0:T(8,128)(2,1)S(1)} %dynamic-slice_bitcast_fusion), channel_id=1, source_target_pairs={{0,64},{32,96},{64,0},{96,32},{128,192},{160,224},{192,128},{224,1... | collective-permute-start | bytes 786440 | tf_op jit(solution)/shard_map/ppermute | solution.py:158
  39.9 30.8 %copy-start.4 = (bf16[1,256,1024]{2,1,0:T(8,128)(2,1)S(1)}, bf16[1,256,1024]{2,1,0:T(8,128)(2,1)}, u32[]{:S(2)}) copy-start(bf16[1,256,1024]{2,1,0:T(8,128)(2,1)} %param.8) | copy-start | bytes 1572868
  39.9 30.8 %copy-start.5 = (bf16[2,1,256,128]{3,2,1,0:T(8,128)(2,1)S(1)}, bf16[2,1,256,128]{3,2,1,0:T(8,128)(2,1)}, u32[]{:S(2)}) copy-start(bf16[2,1,256,128]{3,2,1,0:T(8,128)(2,1)} %param.9) | copy-start | bytes 393220
  42.6 2.0 %copy-start = (bf16[1024,2048]{1,0:T(8,128)(2,1)}, bf16[1024,2048]{1,0:T(8,128)(2,1)S(1)}, u32[]{:S(2)}) copy-start(bf16[1024,2048]{1,0:T(8,128)(2,1)S(1)} %shard_map.64.refs_1_) | copy-start | bytes 12582916
  52.3 9.3 %collective-permute-start.4 = (bf16[1024,128]{1,0:T(8,128)(2,1)S(1)}, bf16[1024,128]{1,0:T(8,128)(2,1)S(1)}, u32[]{:S(2)}, u32[]{:S(2)}) collective-permute-start(bf16[1024,128]{1,0:T(8,128)(2,1)S(1)} %broadcast_select_fusion.refs_2_), channel_id=1, source_target_pairs={{0,32},{32,0},{64,96},{96,64},{128,160},{160,128},{192,224},{224,1... | collective-permute-start | bytes 786440 | tf_op jit(solution)/shard_map/ppermute | solution.py:267
  55.5 12.6 %collective-permute-start.2 = (bf16[1024,128]{1,0:T(8,128)(2,1)S(1)}, bf16[1024,128]{1,0:T(8,128)(2,1)S(1)}, u32[]{:S(2)}, u32[]{:S(2)}) collective-permute-start(bf16[1024,128]{1,0:T(8,128)(2,1)S(1)} %broadcast_select_fusion.refs_2_), channel_id=1, source_target_pairs={{0,384},{32,416},{64,448},{96,480},{128,0},{160,32},{192,64},{224,... | collective-permute-start | bytes 786440 | tf_op jit(solution)/shard_map/ppermute | solution.py:258
  58.9 18.6 %collective-permute-start.7 = (bf16[1024,128]{1,0:T(8,128)(2,1)S(1)}, bf16[1024,128]{1,0:T(8,128)(2,1)S(1)}, u32[]{:S(2)}, u32[]{:S(2)}) collective-permute-start(bf16[1024,128]{1,0:T(8,128)(2,1)S(1)} %broadcast_select_fusion.refs_2_), channel_id=1, source_target_pairs={{0,128},{32,160},{64,192},{96,224},{128,256},{160,288},{192,320},{... | collective-permute-start | bytes 786440 | tf_op jit(solution)/shard_map/ppermute | solution.py:258
  61.6 13.0 %collective-permute-start.5 = (bf16[1024,128]{1,0:T(8,128)(2,1)S(1)}, bf16[1024,128]{1,0:T(8,128)(2,1)S(1)}, u32[]{:S(2)}, u32[]{:S(2)}) collective-permute-start(bf16[1024,128]{1,0:T(8,128)(2,1)S(1)} %collective-permute-done.4.refs_3_), channel_id=1, source_target_pairs={{0,128},{32,160},{64,192},{96,224},{128,256},{160,288},{192,320},{... | collective-permute-start | bytes 786440 | tf_op jit(solution)/shard_map/ppermute | solution.py:258
  63.5 14.0 %collective-permute-start.8 = (bf16[1024,128]{1,0:T(8,128)(2,1)S(1)}, bf16[1024,128]{1,0:T(8,128)(2,1)S(1)}, u32[]{:S(2)}, u32[]{:S(2)}) collective-permute-start(bf16[1024,128]{1,0:T(8,128)(2,1)S(1)} %collective-permute-done.4.refs_3_), channel_id=1, source_target_pairs={{0,384},{32,416},{64,448},{96,480},{128,0},{160,32},{192,64},{224,... | collective-permute-start | bytes 786440 | tf_op jit(solution)/shard_map/ppermute | solution.py:258
  68.2 15.2 %collective-permute-start.3 = (bf16[1024,128]{1,0:T(8,128)(2,1)S(1)}, bf16[1024,128]{1,0:T(8,128)(2,1)S(1)}, u32[]{:S(2)}, u32[]{:S(2)}) collective-permute-start(bf16[1024,128]{1,0:T(8,128)(2,1)S(1)} %collective-permute-done.2.refs_4_), channel_id=1, source_target_pairs={{0,384},{32,416},{64,448},{96,480},{128,0},{160,32},{192,64},{224,... | collective-permute-start | bytes 786440 | tf_op jit(solution)/shard_map/ppermute | solution.py:258
  74.6 8.8 %collective-permute-start.6 = (bf16[1024,128]{1,0:T(8,128)(2,1)S(1)}, bf16[1024,128]{1,0:T(8,128)(2,1)S(1)}, u32[]{:S(2)}, u32[]{:S(2)}) collective-permute-start(bf16[1024,128]{1,0:T(8,128)(2,1)S(1)} %collective-permute-done.5.refs_3_), channel_id=1, source_target_pairs={{0,128},{32,160},{64,192},{96,224},{128,256},{160,288},{192,320},{... | collective-permute-start | bytes 786440 | tf_op jit(solution)/shard_map/ppermute | solution.py:258
  83.4 11.4 %copy-start.1 = (bf16[1024,2048]{1,0:T(8,128)(2,1)S(1)}, bf16[1024,2048]{1,0:T(8,128)(2,1)}, u32[]{:S(2)}) copy-start(bf16[1024,2048]{1,0:T(8,128)(2,1)} %copy-done) | copy-start | bytes 12582916
  86.8 31.3 %collective-permute-start.11 = (bf16[256,1024]{1,0:T(8,128)(2,1)S(1)}, bf16[256,1024]{1,0:T(8,128)(2,1)S(1)}, u32[]{:S(2)}, u32[]{:S(2)}) collective-permute-start(bf16[256,1024]{1,0:T(8,128)(2,1)S(1)} %shard_map.67.refs_2_), channel_id=1, source_target_pairs={{0,16},{8,24},{16,0},{24,8},{1,17},{9,25},{17,1},{25,9},{2,18},{10... | collective-permute-start | bytes 1572872 | tf_op jit(solution)/shard_map/ppermute | solution.py:254
  96.1 9.1 %collective-permute-start.10 = (bf16[4,256,128]{2,1,0:T(8,128)(2,1)S(1)}, bf16[4,256,128]{2,1,0:T(8,128)(2,1)S(1)}, u32[]{:S(2)}, u32[]{:S(2)}) collective-permute-start(bf16[4,256,128]{2,1,0:T(8,128)(2,1)S(1)} %get-tuple-element.29), channel_id=1, source_target_pairs={{0,7},{1,2},{2,1},{3,4},{4,3},{5,6},{6,5},{7,0},{8,15},{9,10},{10,... | collective-permute-start | bytes 786440 | tf_op jit(solution)/shard_map/ppermute | solution.py:225
  101.2 7.4 %collective-permute-start.9 = (bf16[4,256,128]{2,1,0:T(8,128)(2,1)S(1)}, bf16[4,256,128]{2,1,0:T(8,128)(2,1)S(1)}, u32[]{:S(2)}, u32[]{:S(2)}) collective-permute-start(bf16[4,256,128]{2,1,0:T(8,128)(2,1)S(1)} %get-tuple-element.28), channel_id=1, source_target_pairs={{0,1},{1,0},{2,3},{3,2},{4,5},{5,4},{6,7},{7,6},{8,9},{9,8},{10,11... | collective-permute-start | bytes 786440 | tf_op jit(solution)/shard_map/ppermute | solution.py:224
  109.6 30.5 %all-to-all-start.1 = ((bf16[8,256,128]{2,1,0:T(8,128)(2,1)}), bf16[8,256,128]{2,1,0:T(8,128)(2,1)S(1)}, u32[]{:S(2)}, u32[]{:S(2)}) async-start(bf16[8,256,128]{2,1,0:T(8,128)(2,1)} %bitcast.13), calls=%async_computation.1 | async-start | bytes 1048576 | tf_op jit(solution)/shard_map/all_to_all | solution.py:239
  118.1 2.2 %copy-start.2 = (bf16[1024,2048]{1,0:T(8,128)(2,1)S(1)}, bf16[1024,2048]{1,0:T(8,128)(2,1)}, u32[]{:S(2)}) copy-start(bf16[1024,2048]{1,0:T(8,128)(2,1)} %copy-done) | copy-start | bytes 12582916
  121.6 15.3 %collective-permute-start.12 = (bf16[4,256,128]{2,1,0:T(8,128)(2,1)S(1)}, bf16[4,256,128]{2,1,0:T(8,128)(2,1)S(1)}, u32[]{:S(2)}, u32[]{:S(2)}) collective-permute-start(bf16[4,256,128]{2,1,0:T(8,128)(2,1)S(1)} %get-tuple-element.31), channel_id=1, source_target_pairs={{0,1},{1,0},{2,3},{3,2},{4,5},{5,4},{6,7},{7,6},{8,9},{9,8},{10,11... | collective-permute-start | bytes 786440 | tf_op jit(solution)/shard_map/ppermute | solution.py:224
  124.1 15.0 %collective-permute-start.13 = (bf16[4,256,128]{2,1,0:T(8,128)(2,1)S(1)}, bf16[4,256,128]{2,1,0:T(8,128)(2,1)S(1)}, u32[]{:S(2)}, u32[]{:S(2)}) collective-permute-start(bf16[4,256,128]{2,1,0:T(8,128)(2,1)S(1)} %get-tuple-element.32), channel_id=1, source_target_pairs={{0,7},{1,2},{2,1},{3,4},{4,3},{5,6},{6,5},{7,0},{8,15},{9,10},{10,... | collective-permute-start | bytes 786440 | tf_op jit(solution)/shard_map/ppermute | solution.py:225
  140.0 19.0 %all-to-all-start.2 = ((bf16[8,256,128]{2,1,0:T(8,128)(2,1)}), bf16[8,256,128]{2,1,0:T(8,128)(2,1)S(1)}, u32[]{:S(2)}, u32[]{:S(2)}) async-start(bf16[8,256,128]{2,1,0:T(8,128)(2,1)} %bitcast.15), calls=%async_computation.2 | async-start | bytes 1048576 | tf_op jit(solution)/shard_map/all_to_all | solution.py:239
